TPU v7x, 512 devices: a whole 4x4x16 slice. The times are simulated.
512 devices in a mesh: inj: 4 (over y), blk: 128 (over z, x, core).
Axes of the slice: x: 4, y: 4, z: 16, core: 2. Of those that a mesh axis runs over, the one named last changes fastest.
Arguments:
- tile_values: bfloat16 [1536, 128, 128], P('blk'), may hold values from -0.3125 to 0.3125
- tile_row: int32 [1536], P('blk'), may hold values from 0 to 3
- tile_dest: int32 [1536, 1], P('blk'), may hold values from 0 to 6, as said below
- trans_block: int32 [128, 21], P('blk'), may hold values from 0 to 3
- inj_pores: int32 [256, 8192], P('inj', 'blk'), may hold values from 0 to 511
- final_weight: bfloat16 [256, 65536], P('inj', 'blk'), may hold values from -6 to 6
Outputs:
- sensitivity: bfloat16 [256, 65536], P('inj', 'blk')
- tile_gradient: bfloat16 [1536, 128, 128], P('blk', 'inj')
Inputs may be any that keep to these rules, and one draw needn't show every extreme that they name: `tile_dest`: among the tiles of one index of blk, every value is named by at most 3 tiles, and 0 by exactly 3 tiles.
All inputs are finite; a program needn't handle non-finite values.
Results may differ from a plain program's by a relative error of at most 0.014.
Values may be sent and summed in bfloat16 or wider, within the bound.
A program may use at most 64 MiB of HBM per device.

v0:
```python
import jax
import jax.numpy as jnp
from jax import lax
from jax.sharding import PartitionSpec as P

NEIGH = 6
STEPS = 4


def passed_along(block, axis, distance):
    devices = range(lax.axis_size(axis))
    route = [((i - distance) % len(devices), i) for i in devices]
    return lax.ppermute(block, axis, route)


def offset_of(slot):
    amount = (slot + 1) // 2
    return amount if slot % 2 == 1 else -amount


def shards(tile_values, tile_row, tile_dest, trans_block, inj_pores, final_weight):
    tile_count = tile_values.shape[0]
    block_width = tile_values.shape[1]
    set_count = final_weight.shape[0]
    pore_count = final_weight.shape[1]
    block_count = pore_count // block_width
    send_blocks = trans_block[0]
    slot_count = send_blocks.shape[0]
    neighbours = NEIGH
    capacity = slot_count // (neighbours + 1)
    targets = tile_dest[:, 0]
    ordinal = jnp.arange(tile_count, dtype=jnp.int32)
    earlier = ordinal[:, None] > ordinal[None, :]
    position = jnp.sum(((targets[:, None] == targets[None, :]) & earlier).astype(jnp.int32), axis=1)
    slot_index = targets * capacity + position
    block_ids = jnp.arange(block_count, dtype=jnp.int32)
    row_hot = (tile_row[:, None] == block_ids[None, :]).astype(jnp.float32)
    return_hot = (send_blocks[:, None] == block_ids[None, :]).astype(jnp.bfloat16)
    set_ids = jnp.arange(set_count, dtype=jnp.int32)[:, None]
    initial = jnp.zeros((set_count, pore_count), jnp.float32).at[set_ids, inj_pores].add(1.0)
    state = initial.astype(jnp.bfloat16).reshape(set_count, block_count, block_width)

    def piece_of(buffer, slot):
        return buffer[:, slot * capacity : (slot + 1) * capacity]

    adjoint = final_weight.reshape(set_count, block_count, block_width)
    fetched = [None] * STEPS
    saved_rows = [None] * STEPS
    for timestep in range(STEPS):
        fetch_outgoing = jnp.take(state, send_blocks, axis=1)
        fetch_pieces = [piece_of(fetch_outgoing, 0)]
        for fetch_slot in range(1, neighbours + 1):
            fetch_pieces.append(
                passed_along(piece_of(fetch_outgoing, fetch_slot), "blk", -offset_of(fetch_slot))
            )
        fetch_incoming = jnp.concatenate(fetch_pieces, axis=1)
        columns = jnp.take(fetch_incoming, slot_index, axis=1)
        fetched[timestep] = columns
        if timestep + 1 < STEPS:
            contrib = jnp.einsum(
                "sib,iab->sia", columns, tile_values, preferred_element_type=jnp.float32
            )
            state = jnp.einsum(
                "sia,ic->sca", contrib, row_hot, precision=lax.Precision.HIGHEST
            ).astype(jnp.bfloat16)
    for timestep in reversed(range(STEPS)):
        adjoint_rows = jnp.take(adjoint, tile_row, axis=1)
        saved_rows[timestep] = adjoint_rows
        outgoing = (
            jnp.zeros((set_count, slot_count, block_width), jnp.bfloat16)
            .at[:, slot_index, :]
            .set(
                jnp.einsum(
                    "sia,iab->sib", adjoint_rows, tile_values, preferred_element_type=jnp.float32
                ).astype(jnp.bfloat16)
            )
        )
        send_pieces = [piece_of(outgoing, 0)]
        for send_slot in range(1, neighbours + 1):
            send_pieces.append(
                passed_along(piece_of(outgoing, send_slot), "blk", offset_of(send_slot))
            )
        incoming = jnp.concatenate(send_pieces, axis=1)
        adjoint = jnp.einsum(
            "snb,nc->scb", incoming, return_hot, preferred_element_type=jnp.float32
        ).astype(jnp.bfloat16)
    accum = jnp.zeros((tile_count, block_width, block_width), jnp.float32)
    for timestep in range(STEPS):
        accum = accum + jnp.einsum(
            "sia,sib->iab",
            saved_rows[timestep],
            fetched[timestep],
            preferred_element_type=jnp.float32,
        )
    partial_sum = accum * (1.0 / set_count)
    summed = lax.psum(partial_sum.astype(jnp.bfloat16), "inj").astype(jnp.float32)
    portion = block_width // lax.axis_size("inj")
    mine = lax.dynamic_slice_in_dim(summed, lax.axis_index("inj") * portion, portion, 1)
    return (adjoint.reshape(set_count, pore_count), mine.astype(jnp.bfloat16))


def solution(mesh):
    placed = (
        P("blk", None, None),
        P("blk"),
        P("blk", None),
        P("blk", None),
        P("inj", "blk"),
        P("inj", "blk"),
    )
    return jax.shard_map(
        shards,
        mesh=mesh,
        in_specs=placed,
        out_specs=(P("inj", "blk"), P("blk", "inj", None)),
        check_vma=False,
    )
```

profile of v0, /device:TPU:2, one launch (start us, length us, event | category | flops | bytes accessed | tf_op | source)
XLA Modules:
  0.0 321.5 jit_solution(13132654927025406320)
XLA Ops:
  10.6 1.1 scatter_fusion
  11.9 1.9 collective-permute-start
  13.9 3.6 %collective-permute-start.1 = (bf16[64,3,128]{2,1,0:T(4,128)(2,1)S(1)}, bf16[64,3,128]{2,1,0:T(4,128)(2,1)S(1)}, u32[]{:S(2)}, u32[]{:S(2)}) collective-permute-start(bf16[64,3,128]{2,1,0:T(4,128)(2,1)S(1)} %copy.159), channel_id=1, source_target_pairs={{1,0},{2,1},{3,2},{4,3},{5,4},{6,5},{7,6},{8,7},{9,8},{10,9},{11,1... | collective-permute-start | bytes 147464 | tf_op jit(solution)/shard_map/ppermute | solution.py:13
  17.6 3.4 %collective-permute-start.2 = (bf16[64,3,128]{2,1,0:T(4,128)(2,1)S(1)}, bf16[64,3,128]{2,1,0:T(4,128)(2,1)S(1)}, u32[]{:S(2)}, u32[]{:S(2)}) collective-permute-start(bf16[64,3,128]{2,1,0:T(4,128)(2,1)S(1)} %copy.160), channel_id=1, source_target_pairs={{126,0},{127,1},{0,2},{1,3},{2,4},{3,5},{4,6},{5,7},{6,8},{7,9},{8... | collective-permute-start | bytes 147464 | tf_op jit(solution)/shard_map/ppermute | solution.py:13
  21.0 10.4 %collective-permute-start.3 = (bf16[64,3,128]{2,1,0:T(4,128)(2,1)S(1)}, bf16[64,3,128]{2,1,0:T(4,128)(2,1)S(1)}, u32[]{:S(2)}, u32[]{:S(2)}) collective-permute-start(bf16[64,3,128]{2,1,0:T(4,128)(2,1)S(1)} %copy.161), channel_id=1, source_target_pairs={{2,0},{3,1},{4,2},{5,3},{6,4},{7,5},{8,6},{9,7},{10,8},{11,9},{12,... | collective-permute-start | bytes 147464 | tf_op jit(solution)/shard_map/ppermute | solution.py:13
  31.5 1.9 collective-permute-start.4
  34.9 28.8 %scatter_custom_fusion.4 = f32[32768]{0:T(1024)S(1)} fusion(s32[4096]{0:T(1024)S(1)} %reshape.171, f32[4096]{0:T(1024)S(1)} %broadcast.101, f32[]{:T(128)} %constant.40.clone.1), kind=kCustom, calls=%fused_computation.80 | custom fusion | flops 4096 | bytes 131076
  64.6 7.3 %collective-permute-start.5 = (bf16[64,3,128]{2,1,0:T(4,128)(2,1)S(1)}, bf16[64,3,128]{2,1,0:T(4,128)(2,1)S(1)}, u32[]{:S(2)}, u32[]{:S(2)}) collective-permute-start(bf16[64,3,128]{2,1,0:T(4,128)(2,1)S(1)} %copy.163), channel_id=1, source_target_pairs={{3,0},{4,1},{5,2},{6,3},{7,4},{8,5},{9,6},{10,7},{11,8},{12,9},{13... | collective-permute-start | bytes 147464 | tf_op jit(solution)/shard_map/ppermute | solution.py:13
  71.9 2.0 collective-permute-start.24
  74.0 2.3 collective-permute-start.25
  76.3 7.2 %collective-permute-start.26 = (bf16[64,3,128]{2,0,1:T(8,128)(2,1)S(1)}, bf16[64,3,128]{2,0,1:T(8,128)(2,1)S(1)}, u32[]{:S(2)}, u32[]{:S(2)}) collective-permute-start(bf16[64,3,128]{2,0,1:T(8,128)(2,1)S(1)} %get-tuple-element.31), channel_id=1, source_target_pairs={{2,0},{3,1},{4,2},{5,3},{6,4},{7,5},{8,6},{9,7},{10,8},{11,9},{12,... | collective-permute-start | bytes 147464 | tf_op jit(solution)/shard_map/ppermute | solution.py:13
  83.6 1.9 collective-permute-start.27
  85.5 10.1 %collective-permute-start.28 = (bf16[64,3,128]{2,0,1:T(8,128)(2,1)S(1)}, bf16[64,3,128]{2,0,1:T(8,128)(2,1)S(1)}, u32[]{:S(2)}, u32[]{:S(2)}) collective-permute-start(bf16[64,3,128]{2,0,1:T(8,128)(2,1)S(1)} %get-tuple-element.29), channel_id=1, source_target_pairs={{3,0},{4,1},{5,2},{6,3},{7,4},{8,5},{9,6},{10,7},{11,8},{12,9},{13... | collective-permute-start | bytes 147464 | tf_op jit(solution)/shard_map/ppermute | solution.py:13
  95.6 1.3 concatenate.27
  98.1 1.1 scatter_fusion.1
  99.3 1.9 collective-permute-start.29
  101.3 1.9 collective-permute-start.6
  103.3 3.6 %collective-permute-start.7 = (bf16[64,3,128]{2,1,0:T(4,128)(2,1)S(1)}, bf16[64,3,128]{2,1,0:T(4,128)(2,1)S(1)}, u32[]{:S(2)}, u32[]{:S(2)}) collective-permute-start(bf16[64,3,128]{2,1,0:T(4,128)(2,1)S(1)} %copy.166), channel_id=1, source_target_pairs={{1,0},{2,1},{3,2},{4,3},{5,4},{6,5},{7,6},{8,7},{9,8},{10,9},{11,1... | collective-permute-start | bytes 147464 | tf_op jit(solution)/shard_map/ppermute | solution.py:13
  107.1 1.9 collective-permute-start.8
  109.1 6.7 %collective-permute-start.9 = (bf16[64,3,128]{2,1,0:T(4,128)(2,1)S(1)}, bf16[64,3,128]{2,1,0:T(4,128)(2,1)S(1)}, u32[]{:S(2)}, u32[]{:S(2)}) collective-permute-start(bf16[64,3,128]{2,1,0:T(4,128)(2,1)S(1)} %copy.168), channel_id=1, source_target_pairs={{2,0},{3,1},{4,2},{5,3},{6,4},{7,5},{8,6},{9,7},{10,8},{11,9},{12,... | collective-permute-start | bytes 147464 | tf_op jit(solution)/shard_map/ppermute | solution.py:13
  115.8 1.9 collective-permute-start.10
  120.1 7.3 %collective-permute-start.11 = (bf16[64,3,128]{2,1,0:T(4,128)(2,1)S(1)}, bf16[64,3,128]{2,1,0:T(4,128)(2,1)S(1)}, u32[]{:S(2)}, u32[]{:S(2)}) collective-permute-start(bf16[64,3,128]{2,1,0:T(4,128)(2,1)S(1)} %copy.170), channel_id=1, source_target_pairs={{3,0},{4,1},{5,2},{6,3},{7,4},{8,5},{9,6},{10,7},{11,8},{12,9},{13... | collective-permute-start | bytes 147464 | tf_op jit(solution)/shard_map/ppermute | solution.py:13
  127.5 1.9 collective-permute-start.30
  129.4 2.4 collective-permute-start.31
  131.9 7.2 %collective-permute-start.32 = (bf16[64,3,128]{2,0,1:T(8,128)(2,1)S(1)}, bf16[64,3,128]{2,0,1:T(8,128)(2,1)S(1)}, u32[]{:S(2)}, u32[]{:S(2)}) collective-permute-start(bf16[64,3,128]{2,0,1:T(8,128)(2,1)S(1)} %get-tuple-element.24), channel_id=1, source_target_pairs={{2,0},{3,1},{4,2},{5,3},{6,4},{7,5},{8,6},{9,7},{10,8},{11,9},{12,... | collective-permute-start | bytes 147464 | tf_op jit(solution)/shard_map/ppermute | solution.py:13
  139.1 1.9 collective-permute-start.33
  141.1 10.1 %collective-permute-start.34 = (bf16[64,3,128]{2,0,1:T(8,128)(2,1)S(1)}, bf16[64,3,128]{2,0,1:T(8,128)(2,1)S(1)}, u32[]{:S(2)}, u32[]{:S(2)}) collective-permute-start(bf16[64,3,128]{2,0,1:T(8,128)(2,1)S(1)} %get-tuple-element.22), channel_id=1, source_target_pairs={{3,0},{4,1},{5,2},{6,3},{7,4},{8,5},{9,6},{10,7},{11,8},{12,9},{13... | collective-permute-start | bytes 147464 | tf_op jit(solution)/shard_map/ppermute | solution.py:13
  151.2 1.3 concatenate.28
  153.6 1.9 collective-permute-start.35
  155.7 7.0 %collective-permute-done.35 = bf16[64,3,128]{2,0,1:T(8,128)(2,1)S(1)} collective-permute-done((bf16[64,3,128]{2,0,1:T(8,128)(2,1)S(1)}, bf16[64,3,128]{2,0,1:T(8,128)(2,1)S(1)}, u32[]{:S(2)}, u32[]{:S(2)}) %collective-permute-start.35) | collective-permute-done | bytes 49184 | tf_op jit(solution)/shard_map/ppermute | solution.py:13
  164.7 1.1 scatter_fusion.2
  165.9 1.9 collective-permute-start.12
  167.9 3.6 %collective-permute-start.13 = (bf16[64,3,128]{2,1,0:T(4,128)(2,1)S(1)}, bf16[64,3,128]{2,1,0:T(4,128)(2,1)S(1)}, u32[]{:S(2)}, u32[]{:S(2)}) collective-permute-start(bf16[64,3,128]{2,1,0:T(4,128)(2,1)S(1)} %copy.173), channel_id=1, source_target_pairs={{1,0},{2,1},{3,2},{4,3},{5,4},{6,5},{7,6},{8,7},{9,8},{10,9},{11,1... | collective-permute-start | bytes 147464 | tf_op jit(solution)/shard_map/ppermute | solution.py:13
  171.6 1.9 collective-permute-start.14
  173.6 3.9 %collective-permute-start.15 = (bf16[64,3,128]{2,1,0:T(4,128)(2,1)S(1)}, bf16[64,3,128]{2,1,0:T(4,128)(2,1)}, u32[]{:S(2)}, u32[]{:S(2)}) collective-permute-start(bf16[64,3,128]{2,1,0:T(4,128)(2,1)S(1)} %copy.175), channel_id=1, source_target_pairs={{2,0},{3,1},{4,2},{5,3},{6,4},{7,5},{8,6},{9,7},{10,8},{11,9},{12,... | collective-permute-start | bytes 147464 | tf_op jit(solution)/shard_map/ppermute | solution.py:13
  177.6 1.9 collective-permute-start.16
  181.0 7.3 %collective-permute-start.17 = (bf16[64,3,128]{2,1,0:T(4,128)(2,1)S(1)}, bf16[64,3,128]{2,1,0:T(4,128)(2,1)S(1)}, u32[]{:S(2)}, u32[]{:S(2)}) collective-permute-start(bf16[64,3,128]{2,1,0:T(4,128)(2,1)S(1)} %copy.177), channel_id=1, source_target_pairs={{3,0},{4,1},{5,2},{6,3},{7,4},{8,5},{9,6},{10,7},{11,8},{12,9},{13... | collective-permute-start | bytes 147464 | tf_op jit(solution)/shard_map/ppermute | solution.py:13
  188.4 4.4 %collective-permute-start.36 = (bf16[64,3,128]{2,0,1:T(8,128)(2,1)S(1)}, bf16[64,3,128]{2,0,1:T(8,128)(2,1)S(1)}, u32[]{:S(2)}, u32[]{:S(2)}) collective-permute-start(bf16[64,3,128]{2,0,1:T(8,128)(2,1)S(1)} %get-tuple-element.19), channel_id=1, source_target_pairs={{1,0},{2,1},{3,2},{4,3},{5,4},{6,5},{7,6},{8,7},{9,8},{10,9},{11,1... | collective-permute-start | bytes 147464 | tf_op jit(solution)/shard_map/ppermute | solution.py:13
  192.8 1.9 collective-permute-start.37
  194.7 4.3 %collective-permute-start.38 = (bf16[64,3,128]{2,0,1:T(8,128)(2,1)S(1)}, bf16[64,3,128]{2,0,1:T(8,128)(2,1)S(1)}, u32[]{:S(2)}, u32[]{:S(2)}) collective-permute-start(bf16[64,3,128]{2,0,1:T(8,128)(2,1)S(1)} %get-tuple-element.17), channel_id=1, source_target_pairs={{2,0},{3,1},{4,2},{5,3},{6,4},{7,5},{8,6},{9,7},{10,8},{11,9},{12,... | collective-permute-start | bytes 147464 | tf_op jit(solution)/shard_map/ppermute | solution.py:13
  199.1 1.9 collective-permute-start.39
  201.0 10.1 %collective-permute-start.40 = (bf16[64,3,128]{2,0,1:T(8,128)(2,1)S(1)}, bf16[64,3,128]{2,0,1:T(8,128)(2,1)S(1)}, u32[]{:S(2)}, u32[]{:S(2)}) collective-permute-start(bf16[64,3,128]{2,0,1:T(8,128)(2,1)S(1)} %get-tuple-element.15), channel_id=1, source_target_pairs={{3,0},{4,1},{5,2},{6,3},{7,4},{8,5},{9,6},{10,7},{11,8},{12,9},{13... | collective-permute-start | bytes 147464 | tf_op jit(solution)/shard_map/ppermute | solution.py:13
  211.1 3.6 %concatenate.29 = bf16[64,21,128]{2,1,0:T(8,128)(2,1)S(1)} concatenate(bf16[64,3,128]{2,1,0:T(4,128)(2,1)S(1)} %copy.171, bf16[64,3,128]{2,1,0:T(4,128)(2,1)S(1)} %collective-permute-done.12, bf16[64,3,128]{2,1,0:T(4,128)(2,1)S(1)} %collective-permute-done.13, bf16[64,3,128]{2,1,0:T(4,128)(2,1)} %collective-permute-done.14, bf16[64,3,128]{2,1,0:T(4,128)(2,1)} %collective-permute-done.15, ...), dimensions={1} | concatenate | bytes 688128 | tf_op jit(solution)/shard_map/concatenate | solution.py:83
  214.9 2.1 collective-permute-start.41
  217.7 6.2 %collective-permute-done.41 = bf16[64,3,128]{2,0,1:T(8,128)(2,1)S(1)} collective-permute-done((bf16[64,3,128]{2,0,1:T(8,128)(2,1)S(1)}, bf16[64,3,128]{2,0,1:T(8,128)(2,1)S(1)}, u32[]{:S(2)}, u32[]{:S(2)}) %collective-permute-start.41) | collective-permute-done | bytes 49184 | tf_op jit(solution)/shard_map/ppermute | solution.py:13
  227.2 1.9 collective-permute-start.42
  229.4 2.4 collective-permute-start.43
  231.8 2.0 collective-permute-start.44
  233.8 3.9 %collective-permute-start.45 = (bf16[64,3,128]{2,0,1:T(8,128)(2,1)S(1)}, bf16[64,3,128]{2,0,1:T(8,128)(2,1)S(1)}, u32[]{:S(2)}, u32[]{:S(2)}) collective-permute-start(bf16[64,3,128]{2,0,1:T(8,128)(2,1)S(1)} %get-tuple-element.9), channel_id=1, source_target_pairs={{126,0},{127,1},{0,2},{1,3},{2,4},{3,5},{4,6},{5,7},{6,8},{7,9},{8... | collective-permute-start | bytes 147464 | tf_op jit(solution)/shard_map/ppermute | solution.py:13
  237.7 8.6 %collective-permute-start.46 = (bf16[64,3,128]{2,0,1:T(8,128)(2,1)S(1)}, bf16[64,3,128]{2,0,1:T(8,128)(2,1)S(1)}, u32[]{:S(2)}, u32[]{:S(2)}) collective-permute-start(bf16[64,3,128]{2,0,1:T(8,128)(2,1)S(1)} %get-tuple-element.8), channel_id=1, source_target_pairs={{3,0},{4,1},{5,2},{6,3},{7,4},{8,5},{9,6},{10,7},{11,8},{12,9},{13... | collective-permute-start | bytes 147464 | tf_op jit(solution)/shard_map/ppermute | solution.py:13
  246.4 1.1 scatter_fusion.3
  247.6 1.9 collective-permute-start.47
  249.6 7.0 %collective-permute-done.47 = bf16[64,3,128]{2,0,1:T(8,128)(2,1)S(1)} collective-permute-done((bf16[64,3,128]{2,0,1:T(8,128)(2,1)S(1)}, bf16[64,3,128]{2,0,1:T(8,128)(2,1)S(1)}, u32[]{:S(2)}, u32[]{:S(2)}) %collective-permute-start.47) | collective-permute-done | bytes 49184 | tf_op jit(solution)/shard_map/ppermute | solution.py:13
  257.2 1.2 fusion.1
  258.5 1.9 collective-permute-start.18
  260.5 3.6 %collective-permute-start.19 = (bf16[64,3,128]{2,1,0:T(4,128)(2,1)S(1)}, bf16[64,3,128]{2,1,0:T(4,128)(2,1)S(1)}, u32[]{:S(2)}, u32[]{:S(2)}) collective-permute-start(bf16[64,3,128]{2,1,0:T(4,128)(2,1)S(1)} %copy.180), channel_id=1, source_target_pairs={{1,0},{2,1},{3,2},{4,3},{5,4},{6,5},{7,6},{8,7},{9,8},{10,9},{11,1... | collective-permute-start | bytes 147464 | tf_op jit(solution)/shard_map/ppermute | solution.py:13
  264.2 1.9 collective-permute-start.20
  266.2 3.9 %collective-permute-start.21 = (bf16[64,3,128]{2,1,0:T(4,128)(2,1)S(1)}, bf16[64,3,128]{2,1,0:T(4,128)(2,1)S(1)}, u32[]{:S(2)}, u32[]{:S(2)}) collective-permute-start(bf16[64,3,128]{2,1,0:T(4,128)(2,1)S(1)} %copy.182), channel_id=1, source_target_pairs={{2,0},{3,1},{4,2},{5,3},{6,4},{7,5},{8,6},{9,7},{10,8},{11,9},{12,... | collective-permute-start | bytes 147464 | tf_op jit(solution)/shard_map/ppermute | solution.py:13
  270.2 1.9 collective-permute-start.22
  272.1 7.3 %collective-permute-start.23 = (bf16[64,3,128]{2,1,0:T(4,128)(2,1)S(1)}, bf16[64,3,128]{2,1,0:T(4,128)(2,1)S(1)}, u32[]{:S(2)}, u32[]{:S(2)}) collective-permute-start(bf16[64,3,128]{2,1,0:T(4,128)(2,1)S(1)} %copy.184), channel_id=1, source_target_pairs={{3,0},{4,1},{5,2},{6,3},{7,4},{8,5},{9,6},{10,7},{11,8},{12,9},{13... | collective-permute-start | bytes 147464 | tf_op jit(solution)/shard_map/ppermute | solution.py:13
  279.5 1.8 collective-permute-done.23
  281.3 1.3 concatenate.30
  283.5 29.6 %all-reduce.2.cloned.1.call-done = bf16[12,128,128]{2,1,0:T(8,128)(2,1)} async-done(((bf16[12,128,128]{2,1,0:T(8,128)(2,1)}), bf16[12,128,128]{2,1,0:T(8,128)(2,1)}) %all-reduce.2.cloned.1.call-update) | async-done | bytes 393232 | tf_op jit(solution)/shard_map/psum | solution.py:96
  313.1 1.5 convert_convert_fusion
  (200 shorter events, 21.2 us)
Async XLA Ops:
  7.2 3.1 copy-start
  7.2 0.8 copy-start.10
  7.2 305.9 %all-reduce.2.cloned.1.call-start = ((), (), s32[]{:S(2)}) async-start(), calls=%async_computation | async-start | bytes 786432 | tf_op jit(solution)/shard_map/psum | solution.py:96
  7.9 0.7 copy-start.14
  8.8 89.3 %copy-start.7 = (s32[12]{0:T(128)}, s32[12]{0:T(128)S(1)}, u32[]{:S(2)}) copy-start(s32[12]{0:T(128)S(1)} %fusion.36) | copy-start | bytes 148
  11.9 52.7 %collective-permute-start = (bf16[64,3,128]{2,1,0:T(4,128)(2,1)S(1)}, bf16[64,3,128]{2,1,0:T(4,128)(2,1)S(1)}, u32[]{:S(2)}, u32[]{:S(2)}) collective-permute-start(bf16[64,3,128]{2,1,0:T(4,128)(2,1)S(1)} %copy.158), channel_id=1, source_target_pairs={{127,0},{0,1},{1,2},{2,3},{3,4},{4,5},{5,6},{6,7},{7,8},{8,9},{9,1... | collective-permute-start | bytes 147464 | tf_op jit(solution)/shard_map/ppermute | solution.py:13
  13.9 58.1 %collective-permute-start.1 = (bf16[64,3,128]{2,1,0:T(4,128)(2,1)S(1)}, bf16[64,3,128]{2,1,0:T(4,128)(2,1)S(1)}, u32[]{:S(2)}, u32[]{:S(2)}) collective-permute-start(bf16[64,3,128]{2,1,0:T(4,128)(2,1)S(1)} %copy.159), channel_id=1, source_target_pairs={{1,0},{2,1},{3,2},{4,3},{5,4},{6,5},{7,6},{8,7},{9,8},{10,9},{11,1... | collective-permute-start | bytes 147464 | tf_op jit(solution)/shard_map/ppermute | solution.py:13
  17.6 56.4 %collective-permute-start.2 = (bf16[64,3,128]{2,1,0:T(4,128)(2,1)S(1)}, bf16[64,3,128]{2,1,0:T(4,128)(2,1)S(1)}, u32[]{:S(2)}, u32[]{:S(2)}) collective-permute-start(bf16[64,3,128]{2,1,0:T(4,128)(2,1)S(1)} %copy.160), channel_id=1, source_target_pairs={{126,0},{127,1},{0,2},{1,3},{2,4},{3,5},{4,6},{5,7},{6,8},{7,9},{8... | collective-permute-start | bytes 147464 | tf_op jit(solution)/shard_map/ppermute | solution.py:13
  21.0 55.3 %collective-permute-start.3 = (bf16[64,3,128]{2,1,0:T(4,128)(2,1)S(1)}, bf16[64,3,128]{2,1,0:T(4,128)(2,1)S(1)}, u32[]{:S(2)}, u32[]{:S(2)}) collective-permute-start(bf16[64,3,128]{2,1,0:T(4,128)(2,1)S(1)} %copy.161), channel_id=1, source_target_pairs={{2,0},{3,1},{4,2},{5,3},{6,4},{7,5},{8,6},{9,7},{10,8},{11,9},{12,... | collective-permute-start | bytes 147464 | tf_op jit(solution)/shard_map/ppermute | solution.py:13
  31.4 2.0 copy-start.5
  31.4 2.0 copy-start.1
  31.5 52.1 %collective-permute-start.4 = (bf16[64,3,128]{2,1,0:T(4,128)(2,1)S(1)}, bf16[64,3,128]{2,1,0:T(4,128)(2,1)S(1)}, u32[]{:S(2)}, u32[]{:S(2)}) collective-permute-start(bf16[64,3,128]{2,1,0:T(4,128)(2,1)S(1)} %copy.162), channel_id=1, source_target_pairs={{125,0},{126,1},{127,2},{0,3},{1,4},{2,5},{3,6},{4,7},{5,8},{6,9},... | collective-permute-start | bytes 147464 | tf_op jit(solution)/shard_map/ppermute | solution.py:13
  33.4 86.5 %copy-start.3 = (pred[21]{0:T(512)(128)(4,1)}, pred[21]{0:T(512)(128)(4,1)S(1)}, u32[]{:S(2)}) copy-start(pred[21]{0:T(512)(128)(4,1)S(1)} %compare_and_fusion.1) | copy-start | bytes 67
  33.5 0.7 copy-start.13
  34.1 0.7 copy-start.12
  63.8 55.6 %copy-start.2 = (s32[1024]{0:T(1024)}, s32[1024]{0:T(1024)S(1)}, u32[]{:S(2)}) copy-start(s32[1024]{0:T(1024)S(1)} %pad_clamp_fusion.1) | copy-start | bytes 12292
  64.6 20.9 %collective-permute-start.5 = (bf16[64,3,128]{2,1,0:T(4,128)(2,1)S(1)}, bf16[64,3,128]{2,1,0:T(4,128)(2,1)S(1)}, u32[]{:S(2)}, u32[]{:S(2)}) collective-permute-start(bf16[64,3,128]{2,1,0:T(4,128)(2,1)S(1)} %copy.163), channel_id=1, source_target_pairs={{3,0},{4,1},{5,2},{6,3},{7,4},{8,5},{9,6},{10,7},{11,8},{12,9},{13... | collective-permute-start | bytes 147464 | tf_op jit(solution)/shard_map/ppermute | solution.py:13
  71.9 27.3 %collective-permute-start.24 = (bf16[64,3,128]{2,0,1:T(8,128)(2,1)S(1)}, bf16[64,3,128]{2,0,1:T(8,128)(2,1)S(1)}, u32[]{:S(2)}, u32[]{:S(2)}) collective-permute-start(bf16[64,3,128]{2,0,1:T(8,128)(2,1)S(1)} %get-tuple-element.33), channel_id=1, source_target_pairs={{1,0},{2,1},{3,2},{4,3},{5,4},{6,5},{7,6},{8,7},{9,8},{10,9},{11,1... | collective-permute-start | bytes 147464 | tf_op jit(solution)/shard_map/ppermute | solution.py:13
  74.0 27.3 %collective-permute-start.25 = (bf16[64,3,128]{2,0,1:T(8,128)(2,1)S(1)}, bf16[64,3,128]{2,0,1:T(8,128)(2,1)S(1)}, u32[]{:S(2)}, u32[]{:S(2)}) collective-permute-start(bf16[64,3,128]{2,0,1:T(8,128)(2,1)S(1)} %get-tuple-element.32), channel_id=1, source_target_pairs={{127,0},{0,1},{1,2},{2,3},{3,4},{4,5},{5,6},{6,7},{7,8},{8,9},{9,1... | collective-permute-start | bytes 147464 | tf_op jit(solution)/shard_map/ppermute | solution.py:13
  76.3 27.0 %collective-permute-start.26 = (bf16[64,3,128]{2,0,1:T(8,128)(2,1)S(1)}, bf16[64,3,128]{2,0,1:T(8,128)(2,1)S(1)}, u32[]{:S(2)}, u32[]{:S(2)}) collective-permute-start(bf16[64,3,128]{2,0,1:T(8,128)(2,1)S(1)} %get-tuple-element.31), channel_id=1, source_target_pairs={{2,0},{3,1},{4,2},{5,3},{6,4},{7,5},{8,6},{9,7},{10,8},{11,9},{12,... | collective-permute-start | bytes 147464 | tf_op jit(solution)/shard_map/ppermute | solution.py:13
  83.6 23.5 %collective-permute-start.27 = (bf16[64,3,128]{2,0,1:T(8,128)(2,1)S(1)}, bf16[64,3,128]{2,0,1:T(8,128)(2,1)S(1)}, u32[]{:S(2)}, u32[]{:S(2)}) collective-permute-start(bf16[64,3,128]{2,0,1:T(8,128)(2,1)S(1)} %get-tuple-element.30), channel_id=1, source_target_pairs={{126,0},{127,1},{0,2},{1,3},{2,4},{3,5},{4,6},{5,7},{6,8},{7,9},{8... | collective-permute-start | bytes 147464 | tf_op jit(solution)/shard_map/ppermute | solution.py:13
  85.5 23.5 %collective-permute-start.28 = (bf16[64,3,128]{2,0,1:T(8,128)(2,1)S(1)}, bf16[64,3,128]{2,0,1:T(8,128)(2,1)S(1)}, u32[]{:S(2)}, u32[]{:S(2)}) collective-permute-start(bf16[64,3,128]{2,0,1:T(8,128)(2,1)S(1)} %get-tuple-element.29), channel_id=1, source_target_pairs={{3,0},{4,1},{5,2},{6,3},{7,4},{8,5},{9,6},{10,7},{11,8},{12,9},{13... | collective-permute-start | bytes 147464 | tf_op jit(solution)/shard_map/ppermute | solution.py:13
  99.3 16.5 %collective-permute-start.29 = (bf16[64,3,128]{2,0,1:T(8,128)(2,1)S(1)}, bf16[64,3,128]{2,0,1:T(8,128)(2,1)S(1)}, u32[]{:S(2)}, u32[]{:S(2)}) collective-permute-start(bf16[64,3,128]{2,0,1:T(8,128)(2,1)S(1)} %get-tuple-element.28), channel_id=1, source_target_pairs={{125,0},{126,1},{127,2},{0,3},{1,4},{2,5},{3,6},{4,7},{5,8},{6,9},... | collective-permute-start | bytes 147464 | tf_op jit(solution)/shard_map/ppermute | solution.py:13
  101.3 18.8 %collective-permute-start.6 = (bf16[64,3,128]{2,1,0:T(4,128)(2,1)S(1)}, bf16[64,3,128]{2,1,0:T(4,128)(2,1)S(1)}, u32[]{:S(2)}, u32[]{:S(2)}) collective-permute-start(bf16[64,3,128]{2,1,0:T(4,128)(2,1)S(1)} %copy.165), channel_id=1, source_target_pairs={{127,0},{0,1},{1,2},{2,3},{3,4},{4,5},{5,6},{6,7},{7,8},{8,9},{9,1... | collective-permute-start | bytes 147464 | tf_op jit(solution)/shard_map/ppermute | solution.py:13
  103.3 24.2 %collective-permute-start.7 = (bf16[64,3,128]{2,1,0:T(4,128)(2,1)S(1)}, bf16[64,3,128]{2,1,0:T(4,128)(2,1)S(1)}, u32[]{:S(2)}, u32[]{:S(2)}) collective-permute-start(bf16[64,3,128]{2,1,0:T(4,128)(2,1)S(1)} %copy.166), channel_id=1, source_target_pairs={{1,0},{2,1},{3,2},{4,3},{5,4},{6,5},{7,6},{8,7},{9,8},{10,9},{11,1... | collective-permute-start | bytes 147464 | tf_op jit(solution)/shard_map/ppermute | solution.py:13
  107.1 22.4 %collective-permute-start.8 = (bf16[64,3,128]{2,1,0:T(4,128)(2,1)S(1)}, bf16[64,3,128]{2,1,0:T(4,128)(2,1)S(1)}, u32[]{:S(2)}, u32[]{:S(2)}) collective-permute-start(bf16[64,3,128]{2,1,0:T(4,128)(2,1)S(1)} %copy.167), channel_id=1, source_target_pairs={{126,0},{127,1},{0,2},{1,3},{2,4},{3,5},{4,6},{5,7},{6,8},{7,9},{8... | collective-permute-start | bytes 147464 | tf_op jit(solution)/shard_map/ppermute | solution.py:13
  109.1 22.8 %collective-permute-start.9 = (bf16[64,3,128]{2,1,0:T(4,128)(2,1)S(1)}, bf16[64,3,128]{2,1,0:T(4,128)(2,1)S(1)}, u32[]{:S(2)}, u32[]{:S(2)}) collective-permute-start(bf16[64,3,128]{2,1,0:T(4,128)(2,1)S(1)} %copy.168), channel_id=1, source_target_pairs={{2,0},{3,1},{4,2},{5,3},{6,4},{7,5},{8,6},{9,7},{10,8},{11,9},{12,... | collective-permute-start | bytes 147464 | tf_op jit(solution)/shard_map/ppermute | solution.py:13
  115.8 23.3 %collective-permute-start.10 = (bf16[64,3,128]{2,1,0:T(4,128)(2,1)S(1)}, bf16[64,3,128]{2,1,0:T(4,128)(2,1)S(1)}, u32[]{:S(2)}, u32[]{:S(2)}) collective-permute-start(bf16[64,3,128]{2,1,0:T(4,128)(2,1)S(1)} %copy.169), channel_id=1, source_target_pairs={{125,0},{126,1},{127,2},{0,3},{1,4},{2,5},{3,6},{4,7},{5,8},{6,9},... | collective-permute-start | bytes 147464 | tf_op jit(solution)/shard_map/ppermute | solution.py:13
  120.1 20.9 %collective-permute-start.11 = (bf16[64,3,128]{2,1,0:T(4,128)(2,1)S(1)}, bf16[64,3,128]{2,1,0:T(4,128)(2,1)S(1)}, u32[]{:S(2)}, u32[]{:S(2)}) collective-permute-start(bf16[64,3,128]{2,1,0:T(4,128)(2,1)S(1)} %copy.170), channel_id=1, source_target_pairs={{3,0},{4,1},{5,2},{6,3},{7,4},{8,5},{9,6},{10,7},{11,8},{12,9},{13... | collective-permute-start | bytes 147464 | tf_op jit(solution)/shard_map/ppermute | solution.py:13
  127.5 26.1 %collective-permute-start.30 = (bf16[64,3,128]{2,0,1:T(8,128)(2,1)S(1)}, bf16[64,3,128]{2,0,1:T(8,128)(2,1)S(1)}, u32[]{:S(2)}, u32[]{:S(2)}) collective-permute-start(bf16[64,3,128]{2,0,1:T(8,128)(2,1)S(1)} %get-tuple-element.26), channel_id=1, source_target_pairs={{1,0},{2,1},{3,2},{4,3},{5,4},{6,5},{7,6},{8,7},{9,8},{10,9},{11,1... | collective-permute-start | bytes 147464 | tf_op jit(solution)/shard_map/ppermute | solution.py:13
  129.4 26.1 %collective-permute-start.31 = (bf16[64,3,128]{2,0,1:T(8,128)(2,1)S(1)}, bf16[64,3,128]{2,0,1:T(8,128)(2,1)S(1)}, u32[]{:S(2)}, u32[]{:S(2)}) collective-permute-start(bf16[64,3,128]{2,0,1:T(8,128)(2,1)S(1)} %get-tuple-element.25), channel_id=1, source_target_pairs={{127,0},{0,1},{1,2},{2,3},{3,4},{4,5},{5,6},{6,7},{7,8},{8,9},{9,1... | collective-permute-start | bytes 147464 | tf_op jit(solution)/shard_map/ppermute | solution.py:13
  131.9 23.7 %collective-permute-start.32 = (bf16[64,3,128]{2,0,1:T(8,128)(2,1)S(1)}, bf16[64,3,128]{2,0,1:T(8,128)(2,1)S(1)}, u32[]{:S(2)}, u32[]{:S(2)}) collective-permute-start(bf16[64,3,128]{2,0,1:T(8,128)(2,1)S(1)} %get-tuple-element.24), channel_id=1, source_target_pairs={{2,0},{3,1},{4,2},{5,3},{6,4},{7,5},{8,6},{9,7},{10,8},{11,9},{12,... | collective-permute-start | bytes 147464 | tf_op jit(solution)/shard_map/ppermute | solution.py:13
  139.1 16.5 %collective-permute-start.33 = (bf16[64,3,128]{2,0,1:T(8,128)(2,1)S(1)}, bf16[64,3,128]{2,0,1:T(8,128)(2,1)S(1)}, u32[]{:S(2)}, u32[]{:S(2)}) collective-permute-start(bf16[64,3,128]{2,0,1:T(8,128)(2,1)S(1)} %get-tuple-element.23), channel_id=1, source_target_pairs={{126,0},{127,1},{0,2},{1,3},{2,4},{3,5},{4,6},{5,7},{6,8},{7,9},{8... | collective-permute-start | bytes 147464 | tf_op jit(solution)/shard_map/ppermute | solution.py:13
  141.1 14.6 %collective-permute-start.34 = (bf16[64,3,128]{2,0,1:T(8,128)(2,1)S(1)}, bf16[64,3,128]{2,0,1:T(8,128)(2,1)S(1)}, u32[]{:S(2)}, u32[]{:S(2)}) collective-permute-start(bf16[64,3,128]{2,0,1:T(8,128)(2,1)S(1)} %get-tuple-element.22), channel_id=1, source_target_pairs={{3,0},{4,1},{5,2},{6,3},{7,4},{8,5},{9,6},{10,7},{11,8},{12,9},{13... | collective-permute-start | bytes 147464 | tf_op jit(solution)/shard_map/ppermute | solution.py:13
  153.6 9.0 %collective-permute-start.35 = (bf16[64,3,128]{2,0,1:T(8,128)(2,1)S(1)}, bf16[64,3,128]{2,0,1:T(8,128)(2,1)S(1)}, u32[]{:S(2)}, u32[]{:S(2)}) collective-permute-start(bf16[64,3,128]{2,0,1:T(8,128)(2,1)S(1)} %get-tuple-element.21), channel_id=1, source_target_pairs={{125,0},{126,1},{127,2},{0,3},{1,4},{2,5},{3,6},{4,7},{5,8},{6,9},... | collective-permute-start | bytes 147464 | tf_op jit(solution)/shard_map/ppermute | solution.py:13
  164.1 0.7 copy-start.8
  165.9 15.1 %collective-permute-start.12 = (bf16[64,3,128]{2,1,0:T(4,128)(2,1)S(1)}, bf16[64,3,128]{2,1,0:T(4,128)(2,1)S(1)}, u32[]{:S(2)}, u32[]{:S(2)}) collective-permute-start(bf16[64,3,128]{2,1,0:T(4,128)(2,1)S(1)} %copy.172), channel_id=1, source_target_pairs={{127,0},{0,1},{1,2},{2,3},{3,4},{4,5},{5,6},{6,7},{7,8},{8,9},{9,1... | collective-permute-start | bytes 147464 | tf_op jit(solution)/shard_map/ppermute | solution.py:13
  167.9 20.4 %collective-permute-start.13 = (bf16[64,3,128]{2,1,0:T(4,128)(2,1)S(1)}, bf16[64,3,128]{2,1,0:T(4,128)(2,1)S(1)}, u32[]{:S(2)}, u32[]{:S(2)}) collective-permute-start(bf16[64,3,128]{2,1,0:T(4,128)(2,1)S(1)} %copy.173), channel_id=1, source_target_pairs={{1,0},{2,1},{3,2},{4,3},{5,4},{6,5},{7,6},{8,7},{9,8},{10,9},{11,1... | collective-permute-start | bytes 147464 | tf_op jit(solution)/shard_map/ppermute | solution.py:13
  171.6 21.2 %collective-permute-start.14 = (bf16[64,3,128]{2,1,0:T(4,128)(2,1)S(1)}, bf16[64,3,128]{2,1,0:T(4,128)(2,1)}, u32[]{:S(2)}, u32[]{:S(2)}) collective-permute-start(bf16[64,3,128]{2,1,0:T(4,128)(2,1)S(1)} %copy.174), channel_id=1, source_target_pairs={{126,0},{127,1},{0,2},{1,3},{2,4},{3,5},{4,6},{5,7},{6,8},{7,9},{8... | collective-permute-start | bytes 147464 | tf_op jit(solution)/shard_map/ppermute | solution.py:13
  173.6 21.1 %collective-permute-start.15 = (bf16[64,3,128]{2,1,0:T(4,128)(2,1)S(1)}, bf16[64,3,128]{2,1,0:T(4,128)(2,1)}, u32[]{:S(2)}, u32[]{:S(2)}) collective-permute-start(bf16[64,3,128]{2,1,0:T(4,128)(2,1)S(1)} %copy.175), channel_id=1, source_target_pairs={{2,0},{3,1},{4,2},{5,3},{6,4},{7,5},{8,6},{9,7},{10,8},{11,9},{12,... | collective-permute-start | bytes 147464 | tf_op jit(solution)/shard_map/ppermute | solution.py:13
  177.5 2.0 copy-start.11
  177.6 21.5 %collective-permute-start.16 = (bf16[64,3,128]{2,1,0:T(4,128)(2,1)S(1)}, bf16[64,3,128]{2,1,0:T(4,128)(2,1)}, u32[]{:S(2)}, u32[]{:S(2)}) collective-permute-start(bf16[64,3,128]{2,1,0:T(4,128)(2,1)S(1)} %copy.176), channel_id=1, source_target_pairs={{125,0},{126,1},{127,2},{0,3},{1,4},{2,5},{3,6},{4,7},{5,8},{6,9},... | collective-permute-start | bytes 147464 | tf_op jit(solution)/shard_map/ppermute | solution.py:13
  180.1 0.8 copy-start.4
  181.0 20.0 %collective-permute-start.17 = (bf16[64,3,128]{2,1,0:T(4,128)(2,1)S(1)}, bf16[64,3,128]{2,1,0:T(4,128)(2,1)S(1)}, u32[]{:S(2)}, u32[]{:S(2)}) collective-permute-start(bf16[64,3,128]{2,1,0:T(4,128)(2,1)S(1)} %copy.177), channel_id=1, source_target_pairs={{3,0},{4,1},{5,2},{6,3},{7,4},{8,5},{9,6},{10,7},{11,8},{12,9},{13... | collective-permute-start | bytes 147464 | tf_op jit(solution)/shard_map/ppermute | solution.py:13
  188.4 26.5 %collective-permute-start.36 = (bf16[64,3,128]{2,0,1:T(8,128)(2,1)S(1)}, bf16[64,3,128]{2,0,1:T(8,128)(2,1)S(1)}, u32[]{:S(2)}, u32[]{:S(2)}) collective-permute-start(bf16[64,3,128]{2,0,1:T(8,128)(2,1)S(1)} %get-tuple-element.19), channel_id=1, source_target_pairs={{1,0},{2,1},{3,2},{4,3},{5,4},{6,5},{7,6},{8,7},{9,8},{10,9},{11,1... | collective-permute-start | bytes 147464 | tf_op jit(solution)/shard_map/ppermute | solution.py:13
  192.8 24.2 %collective-permute-start.37 = (bf16[64,3,128]{2,0,1:T(8,128)(2,1)S(1)}, bf16[64,3,128]{2,0,1:T(8,128)(2,1)S(1)}, u32[]{:S(2)}, u32[]{:S(2)}) collective-permute-start(bf16[64,3,128]{2,0,1:T(8,128)(2,1)S(1)} %get-tuple-element.18), channel_id=1, source_target_pairs={{127,0},{0,1},{1,2},{2,3},{3,4},{4,5},{5,6},{6,7},{7,8},{8,9},{9,1... | collective-permute-start | bytes 147464 | tf_op jit(solution)/shard_map/ppermute | solution.py:13
  194.7 22.3 %collective-permute-start.38 = (bf16[64,3,128]{2,0,1:T(8,128)(2,1)S(1)}, bf16[64,3,128]{2,0,1:T(8,128)(2,1)S(1)}, u32[]{:S(2)}, u32[]{:S(2)}) collective-permute-start(bf16[64,3,128]{2,0,1:T(8,128)(2,1)S(1)} %get-tuple-element.17), channel_id=1, source_target_pairs={{2,0},{3,1},{4,2},{5,3},{6,4},{7,5},{8,6},{9,7},{10,8},{11,9},{12,... | collective-permute-start | bytes 147464 | tf_op jit(solution)/shard_map/ppermute | solution.py:13
  199.1 18.0 %collective-permute-start.39 = (bf16[64,3,128]{2,0,1:T(8,128)(2,1)S(1)}, bf16[64,3,128]{2,0,1:T(8,128)(2,1)S(1)}, u32[]{:S(2)}, u32[]{:S(2)}) collective-permute-start(bf16[64,3,128]{2,0,1:T(8,128)(2,1)S(1)} %get-tuple-element.16), channel_id=1, source_target_pairs={{126,0},{127,1},{0,2},{1,3},{2,4},{3,5},{4,6},{5,7},{6,8},{7,9},{8... | collective-permute-start | bytes 147464 | tf_op jit(solution)/shard_map/ppermute | solution.py:13
  201.0 13.7 %copy-start.6 = (s32[1,21]{1,0:T(1,128)S(1)}, s32[1,21]{1,0:T(1,128)}, u32[]{:S(2)}) copy-start(s32[1,21]{1,0:T(1,128)} %param.15) | copy-start | bytes 256
  201.0 16.1 %collective-permute-start.40 = (bf16[64,3,128]{2,0,1:T(8,128)(2,1)S(1)}, bf16[64,3,128]{2,0,1:T(8,128)(2,1)S(1)}, u32[]{:S(2)}, u32[]{:S(2)}) collective-permute-start(bf16[64,3,128]{2,0,1:T(8,128)(2,1)S(1)} %get-tuple-element.15), channel_id=1, source_target_pairs={{3,0},{4,1},{5,2},{6,3},{7,4},{8,5},{9,6},{10,7},{11,8},{12,9},{13... | collective-permute-start | bytes 147464 | tf_op jit(solution)/shard_map/ppermute | solution.py:13
  214.9 9.0 %collective-permute-start.41 = (bf16[64,3,128]{2,0,1:T(8,128)(2,1)S(1)}, bf16[64,3,128]{2,0,1:T(8,128)(2,1)S(1)}, u32[]{:S(2)}, u32[]{:S(2)}) collective-permute-start(bf16[64,3,128]{2,0,1:T(8,128)(2,1)S(1)} %get-tuple-element.14), channel_id=1, source_target_pairs={{125,0},{126,1},{127,2},{0,3},{1,4},{2,5},{3,6},{4,7},{5,8},{6,9},... | collective-permute-start | bytes 147464 | tf_op jit(solution)/shard_map/ppermute | solution.py:13
  227.2 20.4 %collective-permute-start.42 = (bf16[64,3,128]{2,0,1:T(8,128)(2,1)S(1)}, bf16[64,3,128]{2,0,1:T(8,128)(2,1)S(1)}, u32[]{:S(2)}, u32[]{:S(2)}) collective-permute-start(bf16[64,3,128]{2,0,1:T(8,128)(2,1)S(1)} %get-tuple-element.12), channel_id=1, source_target_pairs={{1,0},{2,1},{3,2},{4,3},{5,4},{6,5},{7,6},{8,7},{9,8},{10,9},{11,1... | collective-permute-start | bytes 147464 | tf_op jit(solution)/shard_map/ppermute | solution.py:13
  229.4 20.1 %collective-permute-start.43 = (bf16[64,3,128]{2,0,1:T(8,128)(2,1)S(1)}, bf16[64,3,128]{2,0,1:T(8,128)(2,1)S(1)}, u32[]{:S(2)}, u32[]{:S(2)}) collective-permute-start(bf16[64,3,128]{2,0,1:T(8,128)(2,1)S(1)} %get-tuple-element.11), channel_id=1, source_target_pairs={{127,0},{0,1},{1,2},{2,3},{3,4},{4,5},{5,6},{6,7},{7,8},{8,9},{9,1... | collective-permute-start | bytes 147464 | tf_op jit(solution)/shard_map/ppermute | solution.py:13
  231.8 17.7 %collective-permute-start.44 = (bf16[64,3,128]{2,0,1:T(8,128)(2,1)S(1)}, bf16[64,3,128]{2,0,1:T(8,128)(2,1)S(1)}, u32[]{:S(2)}, u32[]{:S(2)}) collective-permute-start(bf16[64,3,128]{2,0,1:T(8,128)(2,1)S(1)} %get-tuple-element.10), channel_id=1, source_target_pairs={{2,0},{3,1},{4,2},{5,3},{6,4},{7,5},{8,6},{9,7},{10,8},{11,9},{12,... | collective-permute-start | bytes 147464 | tf_op jit(solution)/shard_map/ppermute | solution.py:13
  233.8 15.8 %collective-permute-start.45 = (bf16[64,3,128]{2,0,1:T(8,128)(2,1)S(1)}, bf16[64,3,128]{2,0,1:T(8,128)(2,1)S(1)}, u32[]{:S(2)}, u32[]{:S(2)}) collective-permute-start(bf16[64,3,128]{2,0,1:T(8,128)(2,1)S(1)} %get-tuple-element.9), channel_id=1, source_target_pairs={{126,0},{127,1},{0,2},{1,3},{2,4},{3,5},{4,6},{5,7},{6,8},{7,9},{8... | collective-permute-start | bytes 147464 | tf_op jit(solution)/shard_map/ppermute | solution.py:13
  237.7 8.7 %copy-start.9 = (s32[12]{0:T(128)S(1)}, s32[12]{0:T(128)}, u32[]{:S(2)}) copy-start(s32[12]{0:T(128)} %copy-done.7) | copy-start | bytes 148
  237.7 11.9 %collective-permute-start.46 = (bf16[64,3,128]{2,0,1:T(8,128)(2,1)S(1)}, bf16[64,3,128]{2,0,1:T(8,128)(2,1)S(1)}, u32[]{:S(2)}, u32[]{:S(2)}) collective-permute-start(bf16[64,3,128]{2,0,1:T(8,128)(2,1)S(1)} %get-tuple-element.8), channel_id=1, source_target_pairs={{3,0},{4,1},{5,2},{6,3},{7,4},{8,5},{9,6},{10,7},{11,8},{12,9},{13... | collective-permute-start | bytes 147464 | tf_op jit(solution)/shard_map/ppermute | solution.py:13
  247.6 9.0 %collective-permute-start.47 = (bf16[64,3,128]{2,0,1:T(8,128)(2,1)S(1)}, bf16[64,3,128]{2,0,1:T(8,128)(2,1)S(1)}, u32[]{:S(2)}, u32[]{:S(2)}) collective-permute-start(bf16[64,3,128]{2,0,1:T(8,128)(2,1)S(1)} %get-tuple-element.7), channel_id=1, source_target_pairs={{125,0},{126,1},{127,2},{0,3},{1,4},{2,5},{3,6},{4,7},{5,8},{6,9},... | collective-permute-start | bytes 147464 | tf_op jit(solution)/shard_map/ppermute | solution.py:13
  258.5 13.6 %collective-permute-start.18 = (bf16[64,3,128]{2,1,0:T(4,128)(2,1)S(1)}, bf16[64,3,128]{2,1,0:T(4,128)(2,1)S(1)}, u32[]{:S(2)}, u32[]{:S(2)}) collective-permute-start(bf16[64,3,128]{2,1,0:T(4,128)(2,1)S(1)} %copy.179), channel_id=1, source_target_pairs={{127,0},{0,1},{1,2},{2,3},{3,4},{4,5},{5,6},{6,7},{7,8},{8,9},{9,1... | collective-permute-start | bytes 147464 | tf_op jit(solution)/shard_map/ppermute | solution.py:13
  260.5 19.0 %collective-permute-start.19 = (bf16[64,3,128]{2,1,0:T(4,128)(2,1)S(1)}, bf16[64,3,128]{2,1,0:T(4,128)(2,1)S(1)}, u32[]{:S(2)}, u32[]{:S(2)}) collective-permute-start(bf16[64,3,128]{2,1,0:T(4,128)(2,1)S(1)} %copy.180), channel_id=1, source_target_pairs={{1,0},{2,1},{3,2},{4,3},{5,4},{6,5},{7,6},{8,7},{9,8},{10,9},{11,1... | collective-permute-start | bytes 147464 | tf_op jit(solution)/shard_map/ppermute | solution.py:13
  264.2 15.3 %collective-permute-start.20 = (bf16[64,3,128]{2,1,0:T(4,128)(2,1)S(1)}, bf16[64,3,128]{2,1,0:T(4,128)(2,1)S(1)}, u32[]{:S(2)}, u32[]{:S(2)}) collective-permute-start(bf16[64,3,128]{2,1,0:T(4,128)(2,1)S(1)} %copy.181), channel_id=1, source_target_pairs={{126,0},{127,1},{0,2},{1,3},{2,4},{3,5},{4,6},{5,7},{6,8},{7,9},{8... | collective-permute-start | bytes 147464 | tf_op jit(solution)/shard_map/ppermute | solution.py:13
  266.2 13.3 %collective-permute-start.21 = (bf16[64,3,128]{2,1,0:T(4,128)(2,1)S(1)}, bf16[64,3,128]{2,1,0:T(4,128)(2,1)S(1)}, u32[]{:S(2)}, u32[]{:S(2)}) collective-permute-start(bf16[64,3,128]{2,1,0:T(4,128)(2,1)S(1)} %copy.182), channel_id=1, source_target_pairs={{2,0},{3,1},{4,2},{5,3},{6,4},{7,5},{8,6},{9,7},{10,8},{11,9},{12,... | collective-permute-start | bytes 147464 | tf_op jit(solution)/shard_map/ppermute | solution.py:13
  270.2 9.3 %collective-permute-start.22 = (bf16[64,3,128]{2,1,0:T(4,128)(2,1)S(1)}, bf16[64,3,128]{2,1,0:T(4,128)(2,1)S(1)}, u32[]{:S(2)}, u32[]{:S(2)}) collective-permute-start(bf16[64,3,128]{2,1,0:T(4,128)(2,1)S(1)} %copy.183), channel_id=1, source_target_pairs={{125,0},{126,1},{127,2},{0,3},{1,4},{2,5},{3,6},{4,7},{5,8},{6,9},... | collective-permute-start | bytes 147464 | tf_op jit(solution)/shard_map/ppermute | solution.py:13
  272.1 9.1 %collective-permute-start.23 = (bf16[64,3,128]{2,1,0:T(4,128)(2,1)S(1)}, bf16[64,3,128]{2,1,0:T(4,128)(2,1)S(1)}, u32[]{:S(2)}, u32[]{:S(2)}) collective-permute-start(bf16[64,3,128]{2,1,0:T(4,128)(2,1)S(1)} %copy.184), channel_id=1, source_target_pairs={{3,0},{4,1},{5,2},{6,3},{7,4},{8,5},{9,6},{10,7},{11,8},{12,9},{13... | collective-permute-start | bytes 147464 | tf_op jit(solution)/shard_map/ppermute | solution.py:13
Sparse Core Ops, SparseCore 0:
  258.5 54.5 all-reduce.1
where the time goes:
time: 323 us; the launch traced here: 321 us
  starting transfers between devices  189 us (59%)
  waiting for transfers between devices  51.7 us (16%)
  other arithmetic  31.8 us (10%)
  local copies, waits for them, and re-layouts  25.6 us (8%)
  between operations  15.8 us (5%)
  matrix products  7.16 us (2%)
    ppermute x48, starting transfers between devices, passed_along(): return lax.ppermute(block, axis, route)  189 us
    psum x1, waiting for transfers between devices, shards(): lax.psum(partial_sum.astype(jnp.bfloat16), 'inj').astype(jnp.float32)  29.6 us
    unnamed x4, other arithmetic  28.9 us
    ppermute x48, waiting for transfers between devices, passed_along(): return lax.ppermute(block, axis, route)  22 us
    concatenate x4, local copies, waits for them, and re-layouts, shards(): incoming = jnp.concatenate(send_pieces, axis=1)  7.51 us
  transfers between devices with their start and end apart: 49, of which 5 were waited for; matrix products, arithmetic and copies ran while one was open for 15% of the time, Pallas kernels for 0%

commit v1 on v0

--- a/solution.py
+++ b/solution.py
@@ -93,7 +93,12 @@
             preferred_element_type=jnp.float32,
         )
     partial_sum = accum * (1.0 / set_count)
-    summed = lax.psum(partial_sum.astype(jnp.bfloat16), "inj").astype(jnp.float32)
+
+    def _create_entries(slab_in, named_axis):
+        local_now = lax.all_gather(slab_in, named_axis).sum(axis=0)
+        return local_now
+
+    summed = _create_entries(partial_sum.astype(jnp.bfloat16), "inj").astype(jnp.float32)
     portion = block_width // lax.axis_size("inj")
     mine = lax.dynamic_slice_in_dim(summed, lax.axis_index("inj") * portion, portion, 1)
     return (adjoint.reshape(set_count, pore_count), mine.astype(jnp.bfloat16))

time: 323 us -> 299 us (0.926)
  the two profiles are of different devices: /device:TPU:2 before, /device:TPU:1 now
where the time goes in v1:
time: 299 us; the launch traced here: 297 us
  starting transfers between devices  200 us (67%)
  other arithmetic  34.7 us (12%)
  local copies, waits for them, and re-layouts  22.9 us (8%)
  waiting for transfers between devices  16.9 us (6%)
  between operations  15.7 us (5%)
  matrix products  7.11 us (2%)
    ppermute x48, starting transfers between devices, passed_along(): return lax.ppermute(block, axis, route)  200 us
    unnamed x4, other arithmetic  28.9 us
    ppermute x48, waiting for transfers between devices, passed_along(): return lax.ppermute(block, axis, route)  14.1 us
    concatenate x4, local copies, waits for them, and re-layouts, shards(): incoming = jnp.concatenate(send_pieces, axis=1)  7.52 us
  transfers between devices with their start and end apart: 49, of which 6 were waited for; matrix products, arithmetic and copies ran while one was open for 17% of the time, Pallas kernels for 0%

profile of v1, /device:TPU:1, one launch (start us, length us, event | category | flops | bytes accessed | tf_op | source)
XLA Modules:
  0.0 297.4 jit_solution(706017695096365293)
XLA Ops:
  8.6 0.9 convert_reduce_fusion
  12.0 1.1 scatter_fusion
  13.3 4.5 %collective-permute-start = (bf16[64,3,128]{2,1,0:T(4,128)(2,1)S(1)}, bf16[64,3,128]{2,1,0:T(4,128)(2,1)S(1)}, u32[]{:S(2)}, u32[]{:S(2)}) collective-permute-start(bf16[64,3,128]{2,1,0:T(4,128)(2,1)S(1)} %copy.197), channel_id=1, source_target_pairs={{127,0},{0,1},{1,2},{2,3},{3,4},{4,5},{5,6},{6,7},{7,8},{8,9},{9,1... | collective-permute-start | bytes 147464 | tf_op jit(solution)/shard_map/ppermute | solution.py:13
  17.8 6.2 %collective-permute-start.1 = (bf16[64,3,128]{2,1,0:T(4,128)(2,1)S(1)}, bf16[64,3,128]{2,1,0:T(4,128)(2,1)S(1)}, u32[]{:S(2)}, u32[]{:S(2)}) collective-permute-start(bf16[64,3,128]{2,1,0:T(4,128)(2,1)S(1)} %copy.198), channel_id=1, source_target_pairs={{1,0},{2,1},{3,2},{4,3},{5,4},{6,5},{7,6},{8,7},{9,8},{10,9},{11,1... | collective-permute-start | bytes 147464 | tf_op jit(solution)/shard_map/ppermute | solution.py:13
  24.1 1.9 collective-permute-start.2
  26.1 7.9 %collective-permute-start.3 = (bf16[64,3,128]{2,1,0:T(4,128)(2,1)S(1)}, bf16[64,3,128]{2,1,0:T(4,128)(2,1)S(1)}, u32[]{:S(2)}, u32[]{:S(2)}) collective-permute-start(bf16[64,3,128]{2,1,0:T(4,128)(2,1)S(1)} %copy.200), channel_id=1, source_target_pairs={{2,0},{3,1},{4,2},{5,3},{6,4},{7,5},{8,6},{9,7},{10,8},{11,9},{12,... | collective-permute-start | bytes 147464 | tf_op jit(solution)/shard_map/ppermute | solution.py:13
  34.1 1.9 collective-permute-start.4
  36.4 28.8 %scatter_custom_fusion.4 = f32[32768]{0:T(1024)S(1)} fusion(s32[4096]{0:T(1024)S(1)} %reshape.171, f32[4096]{0:T(1024)S(1)} %broadcast.101, f32[]{:T(128)} %constant.14.clone.1), kind=kCustom, calls=%fused_computation.80 | custom fusion | flops 4096 | bytes 131076
  66.0 7.0 %collective-permute-start.5 = (bf16[64,3,128]{2,1,0:T(4,128)(2,1)S(1)}, bf16[64,3,128]{2,1,0:T(4,128)(2,1)S(1)}, u32[]{:S(2)}, u32[]{:S(2)}) collective-permute-start(bf16[64,3,128]{2,1,0:T(4,128)(2,1)S(1)} %copy.202), channel_id=1, source_target_pairs={{3,0},{4,1},{5,2},{6,3},{7,4},{8,5},{9,6},{10,7},{11,8},{12,9},{13... | collective-permute-start | bytes 147464 | tf_op jit(solution)/shard_map/ppermute | solution.py:13
  73.1 7.3 %collective-permute-start.24 = (bf16[64,3,128]{2,0,1:T(8,128)(2,1)S(1)}, bf16[64,3,128]{2,0,1:T(8,128)(2,1)S(1)}, u32[]{:S(2)}, u32[]{:S(2)}) collective-permute-start(bf16[64,3,128]{2,0,1:T(8,128)(2,1)S(1)} %get-tuple-element.33), channel_id=1, source_target_pairs={{1,0},{2,1},{3,2},{4,3},{5,4},{6,5},{7,6},{8,7},{9,8},{10,9},{11,1... | collective-permute-start | bytes 147464 | tf_op jit(solution)/shard_map/ppermute | solution.py:13
  80.4 1.9 collective-permute-start.25
  82.3 6.6 %collective-permute-start.26 = (bf16[64,3,128]{2,0,1:T(8,128)(2,1)S(1)}, bf16[64,3,128]{2,0,1:T(8,128)(2,1)S(1)}, u32[]{:S(2)}, u32[]{:S(2)}) collective-permute-start(bf16[64,3,128]{2,0,1:T(8,128)(2,1)S(1)} %get-tuple-element.31), channel_id=1, source_target_pairs={{2,0},{3,1},{4,2},{5,3},{6,4},{7,5},{8,6},{9,7},{10,8},{11,9},{12,... | collective-permute-start | bytes 147464 | tf_op jit(solution)/shard_map/ppermute | solution.py:13
  88.9 1.9 collective-permute-start.27
  90.8 2.8 collective-permute-start.28
  93.6 1.3 concatenate.27
  96.1 1.1 scatter_fusion.1
  97.3 4.3 %collective-permute-start.29 = (bf16[64,3,128]{2,0,1:T(8,128)(2,1)S(1)}, bf16[64,3,128]{2,0,1:T(8,128)(2,1)S(1)}, u32[]{:S(2)}, u32[]{:S(2)}) collective-permute-start(bf16[64,3,128]{2,0,1:T(8,128)(2,1)S(1)} %get-tuple-element.28), channel_id=1, source_target_pairs={{125,0},{126,1},{127,2},{0,3},{1,4},{2,5},{3,6},{4,7},{5,8},{6,9},... | collective-permute-start | bytes 147464 | tf_op jit(solution)/shard_map/ppermute | solution.py:13
  101.7 4.3 %collective-permute-start.6 = (bf16[64,3,128]{2,1,0:T(4,128)(2,1)S(1)}, bf16[64,3,128]{2,1,0:T(4,128)(2,1)S(1)}, u32[]{:S(2)}, u32[]{:S(2)}) collective-permute-start(bf16[64,3,128]{2,1,0:T(4,128)(2,1)S(1)} %copy.204), channel_id=1, source_target_pairs={{127,0},{0,1},{1,2},{2,3},{3,4},{4,5},{5,6},{6,7},{7,8},{8,9},{9,1... | collective-permute-start | bytes 147464 | tf_op jit(solution)/shard_map/ppermute | solution.py:13
  106.1 1.9 collective-permute-start.7
  108.1 2.0 collective-permute-start.8
  110.2 6.8 %collective-permute-start.9 = (bf16[64,3,128]{2,1,0:T(4,128)(2,1)S(1)}, bf16[64,3,128]{2,1,0:T(4,128)(2,1)S(1)}, u32[]{:S(2)}, u32[]{:S(2)}) collective-permute-start(bf16[64,3,128]{2,1,0:T(4,128)(2,1)S(1)} %copy.207), channel_id=1, source_target_pairs={{2,0},{3,1},{4,2},{5,3},{6,4},{7,5},{8,6},{9,7},{10,8},{11,9},{12,... | collective-permute-start | bytes 147464 | tf_op jit(solution)/shard_map/ppermute | solution.py:13
  117.1 1.9 collective-permute-start.10
  121.4 7.0 %collective-permute-start.11 = (bf16[64,3,128]{2,1,0:T(4,128)(2,1)S(1)}, bf16[64,3,128]{2,1,0:T(4,128)(2,1)S(1)}, u32[]{:S(2)}, u32[]{:S(2)}) collective-permute-start(bf16[64,3,128]{2,1,0:T(4,128)(2,1)S(1)} %copy.209), channel_id=1, source_target_pairs={{3,0},{4,1},{5,2},{6,3},{7,4},{8,5},{9,6},{10,7},{11,8},{12,9},{13... | collective-permute-start | bytes 147464 | tf_op jit(solution)/shard_map/ppermute | solution.py:13
  128.5 7.4 %collective-permute-start.30 = (bf16[64,3,128]{2,0,1:T(8,128)(2,1)S(1)}, bf16[64,3,128]{2,0,1:T(8,128)(2,1)S(1)}, u32[]{:S(2)}, u32[]{:S(2)}) collective-permute-start(bf16[64,3,128]{2,0,1:T(8,128)(2,1)S(1)} %get-tuple-element.26), channel_id=1, source_target_pairs={{1,0},{2,1},{3,2},{4,3},{5,4},{6,5},{7,6},{8,7},{9,8},{10,9},{11,1... | collective-permute-start | bytes 147464 | tf_op jit(solution)/shard_map/ppermute | solution.py:13
  135.9 1.9 collective-permute-start.31
  137.8 6.6 %collective-permute-start.32 = (bf16[64,3,128]{2,0,1:T(8,128)(2,1)S(1)}, bf16[64,3,128]{2,0,1:T(8,128)(2,1)S(1)}, u32[]{:S(2)}, u32[]{:S(2)}) collective-permute-start(bf16[64,3,128]{2,0,1:T(8,128)(2,1)S(1)} %get-tuple-element.24), channel_id=1, source_target_pairs={{2,0},{3,1},{4,2},{5,3},{6,4},{7,5},{8,6},{9,7},{10,8},{11,9},{12,... | collective-permute-start | bytes 147464 | tf_op jit(solution)/shard_map/ppermute | solution.py:13
  144.4 1.9 collective-permute-start.33
  146.4 2.8 collective-permute-start.34
  149.1 1.3 concatenate.28
  151.6 4.3 %collective-permute-start.35 = (bf16[64,3,128]{2,0,1:T(8,128)(2,1)S(1)}, bf16[64,3,128]{2,0,1:T(8,128)(2,1)S(1)}, u32[]{:S(2)}, u32[]{:S(2)}) collective-permute-start(bf16[64,3,128]{2,0,1:T(8,128)(2,1)S(1)} %get-tuple-element.21), channel_id=1, source_target_pairs={{125,0},{126,1},{127,2},{0,3},{1,4},{2,5},{3,6},{4,7},{5,8},{6,9},... | collective-permute-start | bytes 147464 | tf_op jit(solution)/shard_map/ppermute | solution.py:13
  156.0 4.6 %collective-permute-done.35 = bf16[64,3,128]{2,0,1:T(8,128)(2,1)S(1)} collective-permute-done((bf16[64,3,128]{2,0,1:T(8,128)(2,1)S(1)}, bf16[64,3,128]{2,0,1:T(8,128)(2,1)S(1)}, u32[]{:S(2)}, u32[]{:S(2)}) %collective-permute-start.35) | collective-permute-done | bytes 49184 | tf_op jit(solution)/shard_map/ppermute | solution.py:13
  162.1 1.1 scatter_fusion.2
  163.3 6.7 %collective-permute-start.12 = (bf16[64,3,128]{2,1,0:T(4,128)(2,1)S(1)}, bf16[64,3,128]{2,1,0:T(4,128)(2,1)S(1)}, u32[]{:S(2)}, u32[]{:S(2)}) collective-permute-start(bf16[64,3,128]{2,1,0:T(4,128)(2,1)S(1)} %copy.211), channel_id=1, source_target_pairs={{127,0},{0,1},{1,2},{2,3},{3,4},{4,5},{5,6},{6,7},{7,8},{8,9},{9,1... | collective-permute-start | bytes 147464 | tf_op jit(solution)/shard_map/ppermute | solution.py:13
  170.1 1.9 collective-permute-start.13
  172.1 2.0 collective-permute-start.14
  174.2 6.6 %collective-permute-start.15 = (bf16[64,3,128]{2,1,0:T(4,128)(2,1)S(1)}, bf16[64,3,128]{2,1,0:T(4,128)(2,1)}, u32[]{:S(2)}, u32[]{:S(2)}) collective-permute-start(bf16[64,3,128]{2,1,0:T(4,128)(2,1)S(1)} %copy.214), channel_id=1, source_target_pairs={{2,0},{3,1},{4,2},{5,3},{6,4},{7,5},{8,6},{9,7},{10,8},{11,9},{12,... | collective-permute-start | bytes 147464 | tf_op jit(solution)/shard_map/ppermute | solution.py:13
  180.8 1.9 collective-permute-start.16
  184.1 7.0 %collective-permute-start.17 = (bf16[64,3,128]{2,1,0:T(4,128)(2,1)S(1)}, bf16[64,3,128]{2,1,0:T(4,128)(2,1)S(1)}, u32[]{:S(2)}, u32[]{:S(2)}) collective-permute-start(bf16[64,3,128]{2,1,0:T(4,128)(2,1)S(1)} %copy.216), channel_id=1, source_target_pairs={{3,0},{4,1},{5,2},{6,3},{7,4},{8,5},{9,6},{10,7},{11,8},{12,9},{13... | collective-permute-start | bytes 147464 | tf_op jit(solution)/shard_map/ppermute | solution.py:13
  191.1 4.0 %collective-permute-start.36 = (bf16[64,3,128]{2,0,1:T(8,128)(2,1)S(1)}, bf16[64,3,128]{2,0,1:T(8,128)(2,1)S(1)}, u32[]{:S(2)}, u32[]{:S(2)}) collective-permute-start(bf16[64,3,128]{2,0,1:T(8,128)(2,1)S(1)} %get-tuple-element.19), channel_id=1, source_target_pairs={{1,0},{2,1},{3,2},{4,3},{5,4},{6,5},{7,6},{8,7},{9,8},{10,9},{11,1... | collective-permute-start | bytes 147464 | tf_op jit(solution)/shard_map/ppermute | solution.py:13
  195.1 1.9 collective-permute-start.37
  197.0 6.6 %collective-permute-start.38 = (bf16[64,3,128]{2,0,1:T(8,128)(2,1)S(1)}, bf16[64,3,128]{2,0,1:T(8,128)(2,1)S(1)}, u32[]{:S(2)}, u32[]{:S(2)}) collective-permute-start(bf16[64,3,128]{2,0,1:T(8,128)(2,1)S(1)} %get-tuple-element.17), channel_id=1, source_target_pairs={{2,0},{3,1},{4,2},{5,3},{6,4},{7,5},{8,6},{9,7},{10,8},{11,9},{12,... | collective-permute-start | bytes 147464 | tf_op jit(solution)/shard_map/ppermute | solution.py:13
  203.6 1.9 collective-permute-start.39
  205.6 2.8 collective-permute-start.40
  208.3 3.6 %concatenate.29 = bf16[64,21,128]{2,1,0:T(8,128)(2,1)S(1)} concatenate(bf16[64,3,128]{2,1,0:T(4,128)(2,1)S(1)} %copy.210, bf16[64,3,128]{2,1,0:T(4,128)(2,1)S(1)} %collective-permute-done.12, bf16[64,3,128]{2,1,0:T(4,128)(2,1)S(1)} %collective-permute-done.13, bf16[64,3,128]{2,1,0:T(4,128)(2,1)} %collective-permute-done.14, bf16[64,3,128]{2,1,0:T(4,128)(2,1)} %collective-permute-done.15, ...), dimensions={1} | concatenate | bytes 688128 | tf_op jit(solution)/shard_map/concatenate | solution.py:83
  212.1 4.5 %collective-permute-start.41 = (bf16[64,3,128]{2,0,1:T(8,128)(2,1)S(1)}, bf16[64,3,128]{2,0,1:T(8,128)(2,1)S(1)}, u32[]{:S(2)}, u32[]{:S(2)}) collective-permute-start(bf16[64,3,128]{2,0,1:T(8,128)(2,1)S(1)} %get-tuple-element.14), channel_id=1, source_target_pairs={{125,0},{126,1},{127,2},{0,3},{1,4},{2,5},{3,6},{4,7},{5,8},{6,9},... | collective-permute-start | bytes 147464 | tf_op jit(solution)/shard_map/ppermute | solution.py:13
  217.4 3.8 %collective-permute-done.41 = bf16[64,3,128]{2,0,1:T(8,128)(2,1)S(1)} collective-permute-done((bf16[64,3,128]{2,0,1:T(8,128)(2,1)S(1)}, bf16[64,3,128]{2,0,1:T(8,128)(2,1)S(1)}, u32[]{:S(2)}, u32[]{:S(2)}) %collective-permute-start.41) | collective-permute-done | bytes 49184 | tf_op jit(solution)/shard_map/ppermute | solution.py:13
  223.5 2.8 collective-permute-start.42
  227.1 5.8 %collective-permute-start.43 = (bf16[64,3,128]{2,0,1:T(8,128)(2,1)S(1)}, bf16[64,3,128]{2,0,1:T(8,128)(2,1)S(1)}, u32[]{:S(2)}, u32[]{:S(2)}) collective-permute-start(bf16[64,3,128]{2,0,1:T(8,128)(2,1)S(1)} %get-tuple-element.11), channel_id=1, source_target_pairs={{127,0},{0,1},{1,2},{2,3},{3,4},{4,5},{5,6},{6,7},{7,8},{8,9},{9,1... | collective-permute-start | bytes 147464 | tf_op jit(solution)/shard_map/ppermute | solution.py:13
  232.9 5.5 %collective-permute-start.44 = (bf16[64,3,128]{2,0,1:T(8,128)(2,1)S(1)}, bf16[64,3,128]{2,0,1:T(8,128)(2,1)S(1)}, u32[]{:S(2)}, u32[]{:S(2)}) collective-permute-start(bf16[64,3,128]{2,0,1:T(8,128)(2,1)S(1)} %get-tuple-element.10), channel_id=1, source_target_pairs={{2,0},{3,1},{4,2},{5,3},{6,4},{7,5},{8,6},{9,7},{10,8},{11,9},{12,... | collective-permute-start | bytes 147464 | tf_op jit(solution)/shard_map/ppermute | solution.py:13
  238.5 1.9 collective-permute-start.45
  240.4 2.6 collective-permute-start.46
  243.0 4.5 %collective-permute-start.47 = (bf16[64,3,128]{2,0,1:T(8,128)(2,1)S(1)}, bf16[64,3,128]{2,0,1:T(8,128)(2,1)S(1)}, u32[]{:S(2)}, u32[]{:S(2)}) collective-permute-start(bf16[64,3,128]{2,0,1:T(8,128)(2,1)S(1)} %get-tuple-element.7), channel_id=1, source_target_pairs={{125,0},{126,1},{127,2},{0,3},{1,4},{2,5},{3,6},{4,7},{5,8},{6,9},... | collective-permute-start | bytes 147464 | tf_op jit(solution)/shard_map/ppermute | solution.py:13
  247.6 4.4 %collective-permute-done.47 = bf16[64,3,128]{2,0,1:T(8,128)(2,1)S(1)} collective-permute-done((bf16[64,3,128]{2,0,1:T(8,128)(2,1)S(1)}, bf16[64,3,128]{2,0,1:T(8,128)(2,1)S(1)}, u32[]{:S(2)}, u32[]{:S(2)}) %collective-permute-start.47) | collective-permute-done | bytes 49184 | tf_op jit(solution)/shard_map/ppermute | solution.py:13
  252.6 1.2 fusion.1
  254.2 1.1 scatter_fusion.3
  255.4 6.9 %collective-permute-start.18 = (bf16[64,3,128]{2,1,0:T(4,128)(2,1)S(1)}, bf16[64,3,128]{2,1,0:T(4,128)(2,1)S(1)}, u32[]{:S(2)}, u32[]{:S(2)}) collective-permute-start(bf16[64,3,128]{2,1,0:T(4,128)(2,1)S(1)} %copy.218), channel_id=1, source_target_pairs={{127,0},{0,1},{1,2},{2,3},{3,4},{4,5},{5,6},{6,7},{7,8},{8,9},{9,1... | collective-permute-start | bytes 147464 | tf_op jit(solution)/shard_map/ppermute | solution.py:13
  262.3 1.9 collective-permute-start.19
  264.3 2.0 collective-permute-start.20
  266.4 6.6 %collective-permute-start.21 = (bf16[64,3,128]{2,1,0:T(4,128)(2,1)S(1)}, bf16[64,3,128]{2,1,0:T(4,128)(2,1)S(1)}, u32[]{:S(2)}, u32[]{:S(2)}) collective-permute-start(bf16[64,3,128]{2,1,0:T(4,128)(2,1)S(1)} %copy.221), channel_id=1, source_target_pairs={{2,0},{3,1},{4,2},{5,3},{6,4},{7,5},{8,6},{9,7},{10,8},{11,9},{12,... | collective-permute-start | bytes 147464 | tf_op jit(solution)/shard_map/ppermute | solution.py:13
  273.0 1.9 collective-permute-start.22
  275.0 7.0 %collective-permute-start.23 = (bf16[64,3,128]{2,1,0:T(4,128)(2,1)S(1)}, bf16[64,3,128]{2,1,0:T(4,128)(2,1)S(1)}, u32[]{:S(2)}, u32[]{:S(2)}) collective-permute-start(bf16[64,3,128]{2,1,0:T(4,128)(2,1)S(1)} %copy.223), channel_id=1, source_target_pairs={{3,0},{4,1},{5,2},{6,3},{7,4},{8,5},{9,6},{10,7},{11,8},{12,9},{13... | collective-permute-start | bytes 147464 | tf_op jit(solution)/shard_map/ppermute | solution.py:13
  283.3 1.3 concatenate.30
  285.5 2.8 all-gather.3.cloned.1.call-done
  288.2 1.7 reduce_sum.25
  (185 shorter events, 21.5 us)
Async XLA Ops:
  7.2 4.5 %copy-start = (bf16[12,128,128]{2,1,0:T(8,128)(2,1)S(1)}, bf16[12,128,128]{2,1,0:T(8,128)(2,1)}, u32[]{:S(2)}) copy-start(bf16[12,128,128]{2,1,0:T(8,128)(2,1)} %param.12) | copy-start | bytes 1179652
  7.2 281.0 %all-gather.3.cloned.1.call-start = ((), (), s32[]{:S(2)}) async-start(), calls=%async_computation | async-start | bytes 1966080 | tf_op jit(solution)/shard_map/all_gather | solution.py:98
  11.6 24.4 %copy-start.2 = (s32[1,21]{1,0:T(1,128)S(1)}, s32[1,21]{1,0:T(1,128)}, u32[]{:S(2)}) copy-start(s32[1,21]{1,0:T(1,128)} %param.15) | copy-start | bytes 256
  11.6 24.4 %copy-start.1 = (s32[64,64]{1,0:T(8,128)S(1)}, s32[64,64]{1,0:T(8,128)}, u32[]{:S(2)}) copy-start(s32[64,64]{1,0:T(8,128)} %param.16) | copy-start | bytes 49156
  11.7 24.4 %copy-start.5 = (s32[2]{0:T(128)S(1)}, s32[2]{0:T(128)}, u32[]{:S(2)}) copy-start(s32[2]{0:T(128)} %constant.71) | copy-start | bytes 28
  11.7 24.5 %copy-start.4 = (s32[2]{0:T(128)S(1)}, s32[2]{0:T(128)}, u32[]{:S(2)}) copy-start(s32[2]{0:T(128)} %constant.33) | copy-start | bytes 28
  13.3 52.8 %collective-permute-start = (bf16[64,3,128]{2,1,0:T(4,128)(2,1)S(1)}, bf16[64,3,128]{2,1,0:T(4,128)(2,1)S(1)}, u32[]{:S(2)}, u32[]{:S(2)}) collective-permute-start(bf16[64,3,128]{2,1,0:T(4,128)(2,1)S(1)} %copy.197), channel_id=1, source_target_pairs={{127,0},{0,1},{1,2},{2,3},{3,4},{4,5},{5,6},{6,7},{7,8},{8,9},{9,1... | collective-permute-start | bytes 147464 | tf_op jit(solution)/shard_map/ppermute | solution.py:13
  17.8 55.2 %collective-permute-start.1 = (bf16[64,3,128]{2,1,0:T(4,128)(2,1)S(1)}, bf16[64,3,128]{2,1,0:T(4,128)(2,1)S(1)}, u32[]{:S(2)}, u32[]{:S(2)}) collective-permute-start(bf16[64,3,128]{2,1,0:T(4,128)(2,1)S(1)} %copy.198), channel_id=1, source_target_pairs={{1,0},{2,1},{3,2},{4,3},{5,4},{6,5},{7,6},{8,7},{9,8},{10,9},{11,1... | collective-permute-start | bytes 147464 | tf_op jit(solution)/shard_map/ppermute | solution.py:13
  24.1 56.3 %collective-permute-start.2 = (bf16[64,3,128]{2,1,0:T(4,128)(2,1)S(1)}, bf16[64,3,128]{2,1,0:T(4,128)(2,1)S(1)}, u32[]{:S(2)}, u32[]{:S(2)}) collective-permute-start(bf16[64,3,128]{2,1,0:T(4,128)(2,1)S(1)} %copy.199), channel_id=1, source_target_pairs={{126,0},{127,1},{0,2},{1,3},{2,4},{3,5},{4,6},{5,7},{6,8},{7,9},{8... | collective-permute-start | bytes 147464 | tf_op jit(solution)/shard_map/ppermute | solution.py:13
  26.1 56.2 %collective-permute-start.3 = (bf16[64,3,128]{2,1,0:T(4,128)(2,1)S(1)}, bf16[64,3,128]{2,1,0:T(4,128)(2,1)S(1)}, u32[]{:S(2)}, u32[]{:S(2)}) collective-permute-start(bf16[64,3,128]{2,1,0:T(4,128)(2,1)S(1)} %copy.200), channel_id=1, source_target_pairs={{2,0},{3,1},{4,2},{5,3},{6,4},{7,5},{8,6},{9,7},{10,8},{11,9},{12,... | collective-permute-start | bytes 147464 | tf_op jit(solution)/shard_map/ppermute | solution.py:13
  34.0 31.9 %copy-start.6 = (s32[12,1]{0,1:T(1,128)S(1)}, s32[12,1]{0,1:T(1,128)}, u32[]{:S(2)}) copy-start(s32[12,1]{0,1:T(1,128)} %param.14) | copy-start | bytes 148
  34.1 54.8 %collective-permute-start.4 = (bf16[64,3,128]{2,1,0:T(4,128)(2,1)S(1)}, bf16[64,3,128]{2,1,0:T(4,128)(2,1)S(1)}, u32[]{:S(2)}, u32[]{:S(2)}) collective-permute-start(bf16[64,3,128]{2,1,0:T(4,128)(2,1)S(1)} %copy.201), channel_id=1, source_target_pairs={{125,0},{126,1},{127,2},{0,3},{1,4},{2,5},{3,6},{4,7},{5,8},{6,9},... | collective-permute-start | bytes 147464 | tf_op jit(solution)/shard_map/ppermute | solution.py:13
  66.0 24.8 %collective-permute-start.5 = (bf16[64,3,128]{2,1,0:T(4,128)(2,1)S(1)}, bf16[64,3,128]{2,1,0:T(4,128)(2,1)S(1)}, u32[]{:S(2)}, u32[]{:S(2)}) collective-permute-start(bf16[64,3,128]{2,1,0:T(4,128)(2,1)S(1)} %copy.202), channel_id=1, source_target_pairs={{3,0},{4,1},{5,2},{6,3},{7,4},{8,5},{9,6},{10,7},{11,8},{12,9},{13... | collective-permute-start | bytes 147464 | tf_op jit(solution)/shard_map/ppermute | solution.py:13
  73.1 24.2 %collective-permute-start.24 = (bf16[64,3,128]{2,0,1:T(8,128)(2,1)S(1)}, bf16[64,3,128]{2,0,1:T(8,128)(2,1)S(1)}, u32[]{:S(2)}, u32[]{:S(2)}) collective-permute-start(bf16[64,3,128]{2,0,1:T(8,128)(2,1)S(1)} %get-tuple-element.33), channel_id=1, source_target_pairs={{1,0},{2,1},{3,2},{4,3},{5,4},{6,5},{7,6},{8,7},{9,8},{10,9},{11,1... | collective-permute-start | bytes 147464 | tf_op jit(solution)/shard_map/ppermute | solution.py:13
  80.4 21.3 %collective-permute-start.25 = (bf16[64,3,128]{2,0,1:T(8,128)(2,1)S(1)}, bf16[64,3,128]{2,0,1:T(8,128)(2,1)S(1)}, u32[]{:S(2)}, u32[]{:S(2)}) collective-permute-start(bf16[64,3,128]{2,0,1:T(8,128)(2,1)S(1)} %get-tuple-element.32), channel_id=1, source_target_pairs={{127,0},{0,1},{1,2},{2,3},{3,4},{4,5},{5,6},{6,7},{7,8},{8,9},{9,1... | collective-permute-start | bytes 147464 | tf_op jit(solution)/shard_map/ppermute | solution.py:13
  82.3 23.8 %collective-permute-start.26 = (bf16[64,3,128]{2,0,1:T(8,128)(2,1)S(1)}, bf16[64,3,128]{2,0,1:T(8,128)(2,1)S(1)}, u32[]{:S(2)}, u32[]{:S(2)}) collective-permute-start(bf16[64,3,128]{2,0,1:T(8,128)(2,1)S(1)} %get-tuple-element.31), channel_id=1, source_target_pairs={{2,0},{3,1},{4,2},{5,3},{6,4},{7,5},{8,6},{9,7},{10,8},{11,9},{12,... | collective-permute-start | bytes 147464 | tf_op jit(solution)/shard_map/ppermute | solution.py:13
  88.9 19.2 %collective-permute-start.27 = (bf16[64,3,128]{2,0,1:T(8,128)(2,1)S(1)}, bf16[64,3,128]{2,0,1:T(8,128)(2,1)S(1)}, u32[]{:S(2)}, u32[]{:S(2)}) collective-permute-start(bf16[64,3,128]{2,0,1:T(8,128)(2,1)S(1)} %get-tuple-element.30), channel_id=1, source_target_pairs={{126,0},{127,1},{0,2},{1,3},{2,4},{3,5},{4,6},{5,7},{6,8},{7,9},{8... | collective-permute-start | bytes 147464 | tf_op jit(solution)/shard_map/ppermute | solution.py:13
  90.8 19.4 %collective-permute-start.28 = (bf16[64,3,128]{2,0,1:T(8,128)(2,1)S(1)}, bf16[64,3,128]{2,0,1:T(8,128)(2,1)S(1)}, u32[]{:S(2)}, u32[]{:S(2)}) collective-permute-start(bf16[64,3,128]{2,0,1:T(8,128)(2,1)S(1)} %get-tuple-element.29), channel_id=1, source_target_pairs={{3,0},{4,1},{5,2},{6,3},{7,4},{8,5},{9,6},{10,7},{11,8},{12,9},{13... | collective-permute-start | bytes 147464 | tf_op jit(solution)/shard_map/ppermute | solution.py:13
  97.2 22.8 %copy-start.3 = (s32[12]{0:T(128)S(1)}, s32[12]{0:T(128)}, u32[]{:S(2)}) copy-start(s32[12]{0:T(128)} %param.13) | copy-start | bytes 148
  97.3 19.8 %collective-permute-start.29 = (bf16[64,3,128]{2,0,1:T(8,128)(2,1)S(1)}, bf16[64,3,128]{2,0,1:T(8,128)(2,1)S(1)}, u32[]{:S(2)}, u32[]{:S(2)}) collective-permute-start(bf16[64,3,128]{2,0,1:T(8,128)(2,1)S(1)} %get-tuple-element.28), channel_id=1, source_target_pairs={{125,0},{126,1},{127,2},{0,3},{1,4},{2,5},{3,6},{4,7},{5,8},{6,9},... | collective-permute-start | bytes 147464 | tf_op jit(solution)/shard_map/ppermute | solution.py:13
  101.7 19.7 %collective-permute-start.6 = (bf16[64,3,128]{2,1,0:T(4,128)(2,1)S(1)}, bf16[64,3,128]{2,1,0:T(4,128)(2,1)S(1)}, u32[]{:S(2)}, u32[]{:S(2)}) collective-permute-start(bf16[64,3,128]{2,1,0:T(4,128)(2,1)S(1)} %copy.204), channel_id=1, source_target_pairs={{127,0},{0,1},{1,2},{2,3},{3,4},{4,5},{5,6},{6,7},{7,8},{8,9},{9,1... | collective-permute-start | bytes 147464 | tf_op jit(solution)/shard_map/ppermute | solution.py:13
  106.1 22.4 %collective-permute-start.7 = (bf16[64,3,128]{2,1,0:T(4,128)(2,1)S(1)}, bf16[64,3,128]{2,1,0:T(4,128)(2,1)S(1)}, u32[]{:S(2)}, u32[]{:S(2)}) collective-permute-start(bf16[64,3,128]{2,1,0:T(4,128)(2,1)S(1)} %copy.205), channel_id=1, source_target_pairs={{1,0},{2,1},{3,2},{4,3},{5,4},{6,5},{7,6},{8,7},{9,8},{10,9},{11,1... | collective-permute-start | bytes 147464 | tf_op jit(solution)/shard_map/ppermute | solution.py:13
  108.1 27.8 %collective-permute-start.8 = (bf16[64,3,128]{2,1,0:T(4,128)(2,1)S(1)}, bf16[64,3,128]{2,1,0:T(4,128)(2,1)S(1)}, u32[]{:S(2)}, u32[]{:S(2)}) collective-permute-start(bf16[64,3,128]{2,1,0:T(4,128)(2,1)S(1)} %copy.206), channel_id=1, source_target_pairs={{126,0},{127,1},{0,2},{1,3},{2,4},{3,5},{4,6},{5,7},{6,8},{7,9},{8... | collective-permute-start | bytes 147464 | tf_op jit(solution)/shard_map/ppermute | solution.py:13
  110.2 27.6 %collective-permute-start.9 = (bf16[64,3,128]{2,1,0:T(4,128)(2,1)S(1)}, bf16[64,3,128]{2,1,0:T(4,128)(2,1)S(1)}, u32[]{:S(2)}, u32[]{:S(2)}) collective-permute-start(bf16[64,3,128]{2,1,0:T(4,128)(2,1)S(1)} %copy.207), channel_id=1, source_target_pairs={{2,0},{3,1},{4,2},{5,3},{6,4},{7,5},{8,6},{9,7},{10,8},{11,9},{12,... | collective-permute-start | bytes 147464 | tf_op jit(solution)/shard_map/ppermute | solution.py:13
  117.1 27.3 %collective-permute-start.10 = (bf16[64,3,128]{2,1,0:T(4,128)(2,1)S(1)}, bf16[64,3,128]{2,1,0:T(4,128)(2,1)S(1)}, u32[]{:S(2)}, u32[]{:S(2)}) collective-permute-start(bf16[64,3,128]{2,1,0:T(4,128)(2,1)S(1)} %copy.208), channel_id=1, source_target_pairs={{125,0},{126,1},{127,2},{0,3},{1,4},{2,5},{3,6},{4,7},{5,8},{6,9},... | collective-permute-start | bytes 147464 | tf_op jit(solution)/shard_map/ppermute | solution.py:13
  121.4 25.0 %collective-permute-start.11 = (bf16[64,3,128]{2,1,0:T(4,128)(2,1)S(1)}, bf16[64,3,128]{2,1,0:T(4,128)(2,1)S(1)}, u32[]{:S(2)}, u32[]{:S(2)}) collective-permute-start(bf16[64,3,128]{2,1,0:T(4,128)(2,1)S(1)} %copy.209), channel_id=1, source_target_pairs={{3,0},{4,1},{5,2},{6,3},{7,4},{8,5},{9,6},{10,7},{11,8},{12,9},{13... | collective-permute-start | bytes 147464 | tf_op jit(solution)/shard_map/ppermute | solution.py:13
  128.5 23.1 %collective-permute-start.30 = (bf16[64,3,128]{2,0,1:T(8,128)(2,1)S(1)}, bf16[64,3,128]{2,0,1:T(8,128)(2,1)S(1)}, u32[]{:S(2)}, u32[]{:S(2)}) collective-permute-start(bf16[64,3,128]{2,0,1:T(8,128)(2,1)S(1)} %get-tuple-element.26), channel_id=1, source_target_pairs={{1,0},{2,1},{3,2},{4,3},{5,4},{6,5},{7,6},{8,7},{9,8},{10,9},{11,1... | collective-permute-start | bytes 147464 | tf_op jit(solution)/shard_map/ppermute | solution.py:13
  135.9 20.0 %collective-permute-start.31 = (bf16[64,3,128]{2,0,1:T(8,128)(2,1)S(1)}, bf16[64,3,128]{2,0,1:T(8,128)(2,1)S(1)}, u32[]{:S(2)}, u32[]{:S(2)}) collective-permute-start(bf16[64,3,128]{2,0,1:T(8,128)(2,1)S(1)} %get-tuple-element.25), channel_id=1, source_target_pairs={{127,0},{0,1},{1,2},{2,3},{3,4},{4,5},{5,6},{6,7},{7,8},{8,9},{9,1... | collective-permute-start | bytes 147464 | tf_op jit(solution)/shard_map/ppermute | solution.py:13
  137.8 18.1 %collective-permute-start.32 = (bf16[64,3,128]{2,0,1:T(8,128)(2,1)S(1)}, bf16[64,3,128]{2,0,1:T(8,128)(2,1)S(1)}, u32[]{:S(2)}, u32[]{:S(2)}) collective-permute-start(bf16[64,3,128]{2,0,1:T(8,128)(2,1)S(1)} %get-tuple-element.24), channel_id=1, source_target_pairs={{2,0},{3,1},{4,2},{5,3},{6,4},{7,5},{8,6},{9,7},{10,8},{11,9},{12,... | collective-permute-start | bytes 147464 | tf_op jit(solution)/shard_map/ppermute | solution.py:13
  144.4 11.5 %collective-permute-start.33 = (bf16[64,3,128]{2,0,1:T(8,128)(2,1)S(1)}, bf16[64,3,128]{2,0,1:T(8,128)(2,1)S(1)}, u32[]{:S(2)}, u32[]{:S(2)}) collective-permute-start(bf16[64,3,128]{2,0,1:T(8,128)(2,1)S(1)} %get-tuple-element.23), channel_id=1, source_target_pairs={{126,0},{127,1},{0,2},{1,3},{2,4},{3,5},{4,6},{5,7},{6,8},{7,9},{8... | collective-permute-start | bytes 147464 | tf_op jit(solution)/shard_map/ppermute | solution.py:13
  146.4 9.6 %collective-permute-start.34 = (bf16[64,3,128]{2,0,1:T(8,128)(2,1)S(1)}, bf16[64,3,128]{2,0,1:T(8,128)(2,1)S(1)}, u32[]{:S(2)}, u32[]{:S(2)}) collective-permute-start(bf16[64,3,128]{2,0,1:T(8,128)(2,1)S(1)} %get-tuple-element.22), channel_id=1, source_target_pairs={{3,0},{4,1},{5,2},{6,3},{7,4},{8,5},{9,6},{10,7},{11,8},{12,9},{13... | collective-permute-start | bytes 147464 | tf_op jit(solution)/shard_map/ppermute | solution.py:13
  151.6 9.0 %collective-permute-start.35 = (bf16[64,3,128]{2,0,1:T(8,128)(2,1)S(1)}, bf16[64,3,128]{2,0,1:T(8,128)(2,1)S(1)}, u32[]{:S(2)}, u32[]{:S(2)}) collective-permute-start(bf16[64,3,128]{2,0,1:T(8,128)(2,1)S(1)} %get-tuple-element.21), channel_id=1, source_target_pairs={{125,0},{126,1},{127,2},{0,3},{1,4},{2,5},{3,6},{4,7},{5,8},{6,9},... | collective-permute-start | bytes 147464 | tf_op jit(solution)/shard_map/ppermute | solution.py:13
  163.3 20.7 %collective-permute-start.12 = (bf16[64,3,128]{2,1,0:T(4,128)(2,1)S(1)}, bf16[64,3,128]{2,1,0:T(4,128)(2,1)S(1)}, u32[]{:S(2)}, u32[]{:S(2)}) collective-permute-start(bf16[64,3,128]{2,1,0:T(4,128)(2,1)S(1)} %copy.211), channel_id=1, source_target_pairs={{127,0},{0,1},{1,2},{2,3},{3,4},{4,5},{5,6},{6,7},{7,8},{8,9},{9,1... | collective-permute-start | bytes 147464 | tf_op jit(solution)/shard_map/ppermute | solution.py:13
  170.1 21.0 %collective-permute-start.13 = (bf16[64,3,128]{2,1,0:T(4,128)(2,1)S(1)}, bf16[64,3,128]{2,1,0:T(4,128)(2,1)S(1)}, u32[]{:S(2)}, u32[]{:S(2)}) collective-permute-start(bf16[64,3,128]{2,1,0:T(4,128)(2,1)S(1)} %copy.212), channel_id=1, source_target_pairs={{1,0},{2,1},{3,2},{4,3},{5,4},{6,5},{7,6},{8,7},{9,8},{10,9},{11,1... | collective-permute-start | bytes 147464 | tf_op jit(solution)/shard_map/ppermute | solution.py:13
  172.1 23.0 %collective-permute-start.14 = (bf16[64,3,128]{2,1,0:T(4,128)(2,1)S(1)}, bf16[64,3,128]{2,1,0:T(4,128)(2,1)}, u32[]{:S(2)}, u32[]{:S(2)}) collective-permute-start(bf16[64,3,128]{2,1,0:T(4,128)(2,1)S(1)} %copy.213), channel_id=1, source_target_pairs={{126,0},{127,1},{0,2},{1,3},{2,4},{3,5},{4,6},{5,7},{6,8},{7,9},{8... | collective-permute-start | bytes 147464 | tf_op jit(solution)/shard_map/ppermute | solution.py:13
  174.2 22.9 %collective-permute-start.15 = (bf16[64,3,128]{2,1,0:T(4,128)(2,1)S(1)}, bf16[64,3,128]{2,1,0:T(4,128)(2,1)}, u32[]{:S(2)}, u32[]{:S(2)}) collective-permute-start(bf16[64,3,128]{2,1,0:T(4,128)(2,1)S(1)} %copy.214), channel_id=1, source_target_pairs={{2,0},{3,1},{4,2},{5,3},{6,4},{7,5},{8,6},{9,7},{10,8},{11,9},{12,... | collective-permute-start | bytes 147464 | tf_op jit(solution)/shard_map/ppermute | solution.py:13
  180.8 22.8 %collective-permute-start.16 = (bf16[64,3,128]{2,1,0:T(4,128)(2,1)S(1)}, bf16[64,3,128]{2,1,0:T(4,128)(2,1)}, u32[]{:S(2)}, u32[]{:S(2)}) collective-permute-start(bf16[64,3,128]{2,1,0:T(4,128)(2,1)S(1)} %copy.215), channel_id=1, source_target_pairs={{125,0},{126,1},{127,2},{0,3},{1,4},{2,5},{3,6},{4,7},{5,8},{6,9},... | collective-permute-start | bytes 147464 | tf_op jit(solution)/shard_map/ppermute | solution.py:13
  184.1 21.5 %collective-permute-start.17 = (bf16[64,3,128]{2,1,0:T(4,128)(2,1)S(1)}, bf16[64,3,128]{2,1,0:T(4,128)(2,1)S(1)}, u32[]{:S(2)}, u32[]{:S(2)}) collective-permute-start(bf16[64,3,128]{2,1,0:T(4,128)(2,1)S(1)} %copy.216), channel_id=1, source_target_pairs={{3,0},{4,1},{5,2},{6,3},{7,4},{8,5},{9,6},{10,7},{11,8},{12,9},{13... | collective-permute-start | bytes 147464 | tf_op jit(solution)/shard_map/ppermute | solution.py:13
  191.1 21.0 %collective-permute-start.36 = (bf16[64,3,128]{2,0,1:T(8,128)(2,1)S(1)}, bf16[64,3,128]{2,0,1:T(8,128)(2,1)S(1)}, u32[]{:S(2)}, u32[]{:S(2)}) collective-permute-start(bf16[64,3,128]{2,0,1:T(8,128)(2,1)S(1)} %get-tuple-element.19), channel_id=1, source_target_pairs={{1,0},{2,1},{3,2},{4,3},{5,4},{6,5},{7,6},{8,7},{9,8},{10,9},{11,1... | collective-permute-start | bytes 147464 | tf_op jit(solution)/shard_map/ppermute | solution.py:13
  195.1 21.5 %collective-permute-start.37 = (bf16[64,3,128]{2,0,1:T(8,128)(2,1)S(1)}, bf16[64,3,128]{2,0,1:T(8,128)(2,1)S(1)}, u32[]{:S(2)}, u32[]{:S(2)}) collective-permute-start(bf16[64,3,128]{2,0,1:T(8,128)(2,1)S(1)} %get-tuple-element.18), channel_id=1, source_target_pairs={{127,0},{0,1},{1,2},{2,3},{3,4},{4,5},{5,6},{6,7},{7,8},{8,9},{9,1... | collective-permute-start | bytes 147464 | tf_op jit(solution)/shard_map/ppermute | solution.py:13
  197.0 19.6 %collective-permute-start.38 = (bf16[64,3,128]{2,0,1:T(8,128)(2,1)S(1)}, bf16[64,3,128]{2,0,1:T(8,128)(2,1)S(1)}, u32[]{:S(2)}, u32[]{:S(2)}) collective-permute-start(bf16[64,3,128]{2,0,1:T(8,128)(2,1)S(1)} %get-tuple-element.17), channel_id=1, source_target_pairs={{2,0},{3,1},{4,2},{5,3},{6,4},{7,5},{8,6},{9,7},{10,8},{11,9},{12,... | collective-permute-start | bytes 147464 | tf_op jit(solution)/shard_map/ppermute | solution.py:13
  203.6 13.1 %collective-permute-start.39 = (bf16[64,3,128]{2,0,1:T(8,128)(2,1)S(1)}, bf16[64,3,128]{2,0,1:T(8,128)(2,1)S(1)}, u32[]{:S(2)}, u32[]{:S(2)}) collective-permute-start(bf16[64,3,128]{2,0,1:T(8,128)(2,1)S(1)} %get-tuple-element.16), channel_id=1, source_target_pairs={{126,0},{127,1},{0,2},{1,3},{2,4},{3,5},{4,6},{5,7},{6,8},{7,9},{8... | collective-permute-start | bytes 147464 | tf_op jit(solution)/shard_map/ppermute | solution.py:13
  205.6 11.1 %collective-permute-start.40 = (bf16[64,3,128]{2,0,1:T(8,128)(2,1)S(1)}, bf16[64,3,128]{2,0,1:T(8,128)(2,1)S(1)}, u32[]{:S(2)}, u32[]{:S(2)}) collective-permute-start(bf16[64,3,128]{2,0,1:T(8,128)(2,1)S(1)} %get-tuple-element.15), channel_id=1, source_target_pairs={{3,0},{4,1},{5,2},{6,3},{7,4},{8,5},{9,6},{10,7},{11,8},{12,9},{13... | collective-permute-start | bytes 147464 | tf_op jit(solution)/shard_map/ppermute | solution.py:13
  212.1 9.0 %collective-permute-start.41 = (bf16[64,3,128]{2,0,1:T(8,128)(2,1)S(1)}, bf16[64,3,128]{2,0,1:T(8,128)(2,1)S(1)}, u32[]{:S(2)}, u32[]{:S(2)}) collective-permute-start(bf16[64,3,128]{2,0,1:T(8,128)(2,1)S(1)} %get-tuple-element.14), channel_id=1, source_target_pairs={{125,0},{126,1},{127,2},{0,3},{1,4},{2,5},{3,6},{4,7},{5,8},{6,9},... | collective-permute-start | bytes 147464 | tf_op jit(solution)/shard_map/ppermute | solution.py:13
  223.5 19.5 %collective-permute-start.42 = (bf16[64,3,128]{2,0,1:T(8,128)(2,1)S(1)}, bf16[64,3,128]{2,0,1:T(8,128)(2,1)S(1)}, u32[]{:S(2)}, u32[]{:S(2)}) collective-permute-start(bf16[64,3,128]{2,0,1:T(8,128)(2,1)S(1)} %get-tuple-element.12), channel_id=1, source_target_pairs={{1,0},{2,1},{3,2},{4,3},{5,4},{6,5},{7,6},{8,7},{9,8},{10,9},{11,1... | collective-permute-start | bytes 147464 | tf_op jit(solution)/shard_map/ppermute | solution.py:13
  227.1 20.4 %collective-permute-start.43 = (bf16[64,3,128]{2,0,1:T(8,128)(2,1)S(1)}, bf16[64,3,128]{2,0,1:T(8,128)(2,1)S(1)}, u32[]{:S(2)}, u32[]{:S(2)}) collective-permute-start(bf16[64,3,128]{2,0,1:T(8,128)(2,1)S(1)} %get-tuple-element.11), channel_id=1, source_target_pairs={{127,0},{0,1},{1,2},{2,3},{3,4},{4,5},{5,6},{6,7},{7,8},{8,9},{9,1... | collective-permute-start | bytes 147464 | tf_op jit(solution)/shard_map/ppermute | solution.py:13
  232.9 14.6 %collective-permute-start.44 = (bf16[64,3,128]{2,0,1:T(8,128)(2,1)S(1)}, bf16[64,3,128]{2,0,1:T(8,128)(2,1)S(1)}, u32[]{:S(2)}, u32[]{:S(2)}) collective-permute-start(bf16[64,3,128]{2,0,1:T(8,128)(2,1)S(1)} %get-tuple-element.10), channel_id=1, source_target_pairs={{2,0},{3,1},{4,2},{5,3},{6,4},{7,5},{8,6},{9,7},{10,8},{11,9},{12,... | collective-permute-start | bytes 147464 | tf_op jit(solution)/shard_map/ppermute | solution.py:13
  238.5 9.1 %collective-permute-start.45 = (bf16[64,3,128]{2,0,1:T(8,128)(2,1)S(1)}, bf16[64,3,128]{2,0,1:T(8,128)(2,1)S(1)}, u32[]{:S(2)}, u32[]{:S(2)}) collective-permute-start(bf16[64,3,128]{2,0,1:T(8,128)(2,1)S(1)} %get-tuple-element.9), channel_id=1, source_target_pairs={{126,0},{127,1},{0,2},{1,3},{2,4},{3,5},{4,6},{5,7},{6,8},{7,9},{8... | collective-permute-start | bytes 147464 | tf_op jit(solution)/shard_map/ppermute | solution.py:13
  240.4 7.2 %collective-permute-start.46 = (bf16[64,3,128]{2,0,1:T(8,128)(2,1)S(1)}, bf16[64,3,128]{2,0,1:T(8,128)(2,1)S(1)}, u32[]{:S(2)}, u32[]{:S(2)}) collective-permute-start(bf16[64,3,128]{2,0,1:T(8,128)(2,1)S(1)} %get-tuple-element.8), channel_id=1, source_target_pairs={{3,0},{4,1},{5,2},{6,3},{7,4},{8,5},{9,6},{10,7},{11,8},{12,9},{13... | collective-permute-start | bytes 147464 | tf_op jit(solution)/shard_map/ppermute | solution.py:13
  243.0 9.0 %collective-permute-start.47 = (bf16[64,3,128]{2,0,1:T(8,128)(2,1)S(1)}, bf16[64,3,128]{2,0,1:T(8,128)(2,1)S(1)}, u32[]{:S(2)}, u32[]{:S(2)}) collective-permute-start(bf16[64,3,128]{2,0,1:T(8,128)(2,1)S(1)} %get-tuple-element.7), channel_id=1, source_target_pairs={{125,0},{126,1},{127,2},{0,3},{1,4},{2,5},{3,6},{4,7},{5,8},{6,9},... | collective-permute-start | bytes 147464 | tf_op jit(solution)/shard_map/ppermute | solution.py:13
  255.4 19.6 %collective-permute-start.18 = (bf16[64,3,128]{2,1,0:T(4,128)(2,1)S(1)}, bf16[64,3,128]{2,1,0:T(4,128)(2,1)S(1)}, u32[]{:S(2)}, u32[]{:S(2)}) collective-permute-start(bf16[64,3,128]{2,1,0:T(4,128)(2,1)S(1)} %copy.218), channel_id=1, source_target_pairs={{127,0},{0,1},{1,2},{2,3},{3,4},{4,5},{5,6},{6,7},{7,8},{8,9},{9,1... | collective-permute-start | bytes 147464 | tf_op jit(solution)/shard_map/ppermute | solution.py:13
  262.3 19.7 %collective-permute-start.19 = (bf16[64,3,128]{2,1,0:T(4,128)(2,1)S(1)}, bf16[64,3,128]{2,1,0:T(4,128)(2,1)S(1)}, u32[]{:S(2)}, u32[]{:S(2)}) collective-permute-start(bf16[64,3,128]{2,1,0:T(4,128)(2,1)S(1)} %copy.219), channel_id=1, source_target_pairs={{1,0},{2,1},{3,2},{4,3},{5,4},{6,5},{7,6},{8,7},{9,8},{10,9},{11,1... | collective-permute-start | bytes 147464 | tf_op jit(solution)/shard_map/ppermute | solution.py:13
  264.3 17.8 %collective-permute-start.20 = (bf16[64,3,128]{2,1,0:T(4,128)(2,1)S(1)}, bf16[64,3,128]{2,1,0:T(4,128)(2,1)S(1)}, u32[]{:S(2)}, u32[]{:S(2)}) collective-permute-start(bf16[64,3,128]{2,1,0:T(4,128)(2,1)S(1)} %copy.220), channel_id=1, source_target_pairs={{126,0},{127,1},{0,2},{1,3},{2,4},{3,5},{4,6},{5,7},{6,8},{7,9},{8... | collective-permute-start | bytes 147464 | tf_op jit(solution)/shard_map/ppermute | solution.py:13
  266.4 15.7 %collective-permute-start.21 = (bf16[64,3,128]{2,1,0:T(4,128)(2,1)S(1)}, bf16[64,3,128]{2,1,0:T(4,128)(2,1)S(1)}, u32[]{:S(2)}, u32[]{:S(2)}) collective-permute-start(bf16[64,3,128]{2,1,0:T(4,128)(2,1)S(1)} %copy.221), channel_id=1, source_target_pairs={{2,0},{3,1},{4,2},{5,3},{6,4},{7,5},{8,6},{9,7},{10,8},{11,9},{12,... | collective-permute-start | bytes 147464 | tf_op jit(solution)/shard_map/ppermute | solution.py:13
  273.0 9.4 %collective-permute-start.22 = (bf16[64,3,128]{2,1,0:T(4,128)(2,1)S(1)}, bf16[64,3,128]{2,1,0:T(4,128)(2,1)S(1)}, u32[]{:S(2)}, u32[]{:S(2)}) collective-permute-start(bf16[64,3,128]{2,1,0:T(4,128)(2,1)S(1)} %copy.222), channel_id=1, source_target_pairs={{125,0},{126,1},{127,2},{0,3},{1,4},{2,5},{3,6},{4,7},{5,8},{6,9},... | collective-permute-start | bytes 147464 | tf_op jit(solution)/shard_map/ppermute | solution.py:13
  275.0 8.3 %collective-permute-start.23 = (bf16[64,3,128]{2,1,0:T(4,128)(2,1)S(1)}, bf16[64,3,128]{2,1,0:T(4,128)(2,1)S(1)}, u32[]{:S(2)}, u32[]{:S(2)}) collective-permute-start(bf16[64,3,128]{2,1,0:T(4,128)(2,1)S(1)} %copy.223), channel_id=1, source_target_pairs={{3,0},{4,1},{5,2},{6,3},{7,4},{8,5},{9,6},{10,7},{11,8},{12,9},{13... | collective-permute-start | bytes 147464 | tf_op jit(solution)/shard_map/ppermute | solution.py:13
Sparse Core Ops, SparseCore 0:
  253.9 34.2 all-gather.2
